TPU v7x, 32 devices: a whole 2x2x4 slice. The times are simulated.
32 devices in a mesh: seq: 4 (over z), head: 8 (over y, x, core).
Axes of the slice: x: 2, y: 2, z: 4, core: 2. Of those that a mesh axis runs over, the one named last changes fastest.
Arguments:
- queries: bfloat16 [4096, 8192], P('seq', 'head'), may hold values from -6 to 6
- keys: bfloat16 [4096, 8192], P('seq', 'head'), may hold values from -1 to 1
- values: bfloat16 [4096, 8192], P('seq', 'head'), may hold values from -40 to 40
- log_decay: float32 [64, 4096], P('head', 'seq'), may hold values from -1 to 0
- gain: float32 [8192], P('head'), may hold values from 0.25 to 1.75
- out_grad: bfloat16 [4096, 8192], P('seq', 'head'), may hold values from -16 to 16
Outputs:
- output: bfloat16 [4096, 8192], P('seq', 'head')
- query_grad: bfloat16 [4096, 8192], P('seq', 'head')
- key_grad: bfloat16 [4096, 8192], P('seq', 'head')
- value_grad: bfloat16 [4096, 8192], P('seq', 'head')
- gain_grad: float32 [8192], P('head')
All inputs are finite; a program needn't handle non-finite values.
Results may differ from a plain program's by a relative error of at most 0.001.
Values sent between devices are 32-bit elements; how exact they have to be, the bound alone decides.
A program may use at most 128 MiB of HBM per device.

v0:
```python
import jax
import jax.numpy as jnp
from jax import lax
from jax.sharding import PartitionSpec as P

epsilon = 1e-06
highest = lax.Precision.HIGHEST


def passed_along(value, axis, steps):
    count = lax.axis_size(axis)
    initial, last = (max(0, -steps), min(count, count - steps))
    return lax.ppermute(value, axis, [(source, source + steps) for source in range(initial, last)])


def to_blocks(matrix, heads_local, block_count, block_rows):
    head_width = matrix.shape[1] // heads_local
    return matrix.reshape(block_count, block_rows, heads_local, head_width).transpose(2, 0, 1, 3)


def from_blocks(blocked):
    heads_local, block_count, block_rows, head_width = blocked.shape
    return blocked.transpose(1, 2, 0, 3).reshape(block_count * block_rows, heads_local * head_width)


def carry_forward(device_decay, device_state):

    def relay_step(iteration, prefix):
        outgoing = jnp.exp(device_decay)[:, None, None] * prefix + device_state
        return passed_along(outgoing, "seq", 1)

    return lax.fori_loop(0, lax.axis_size("seq") - 1, relay_step, jnp.zeros_like(device_state))


def carry_backward(device_decay, device_back):

    def relay_step(iteration, suffix):
        outgoing = jnp.exp(device_decay)[:, None, None] * suffix + device_back
        return passed_along(outgoing, "seq", -1)

    return lax.fori_loop(0, lax.axis_size("seq") - 1, relay_step, jnp.zeros_like(device_back))


def local(queries, keys, values, log_decay, gain, out_grad):
    token_rows, channels = queries.shape
    heads_local = log_decay.shape[0]
    block_rows = min(256, token_rows)
    block_count = token_rows // block_rows
    total_channels = channels * lax.axis_size("head")
    query_narrow = to_blocks(queries, heads_local, block_count, block_rows)
    key_narrow = to_blocks(keys, heads_local, block_count, block_rows)
    query_blocks = query_narrow.astype(jnp.float32)
    key_blocks = key_narrow.astype(jnp.float32)
    value_blocks = to_blocks(values, heads_local, block_count, block_rows).astype(jnp.float32)
    decay_sum = jnp.cumsum(log_decay.reshape(heads_local, block_count, block_rows), axis=2)
    block_total = decay_sum[:, :, -1]
    causal = jnp.arange(block_rows)[:, None] >= jnp.arange(block_rows)[None, :]
    mask_decay = jnp.exp(
        jnp.where(causal, decay_sum[..., :, None] - decay_sum[..., None, :], -1e30)
    )
    from_start = jnp.exp(decay_sum)[..., None]
    to_end = jnp.exp(block_total[..., None] - decay_sum)[..., None]
    scores = (
        jnp.einsum("hnid,hnjd->hnij", query_narrow, key_narrow, preferred_element_type=jnp.float32)
        * mask_decay
    )
    inside = jnp.einsum("hnij,hnjd->hnid", scores, value_blocks, precision=highest)
    own_states = jnp.einsum("hnjd,hnje->hnde", key_blocks * to_end, value_blocks, precision=highest)
    device_decay = jnp.sum(block_total, axis=1)
    device_state = jnp.zeros_like(own_states[:, 0])
    for block_index in range(block_count):
        device_state = (
            jnp.exp(block_total[:, block_index])[:, None, None] * device_state
            + own_states[:, block_index]
        )
    incoming = carry_forward(device_decay, device_state)
    entering = []
    running = incoming
    for block_index in range(block_count):
        entering.append(running)
        running = (
            jnp.exp(block_total[:, block_index])[:, None, None] * running
            + own_states[:, block_index]
        )
    entering = jnp.stack(entering, axis=1)
    attended = inside + from_start * jnp.einsum(
        "hnid,hnde->hnie", query_blocks, entering, precision=highest
    )
    flattened = from_blocks(attended)
    grad_wide = out_grad.astype(jnp.float32)
    normed_grad = grad_wide * gain
    squares = lax.psum(jnp.sum(flattened * flattened, axis=1), "head")
    inverse = 1.0 / jnp.sqrt(squares / total_channels + epsilon)
    normed = flattened * inverse[:, None]
    projected = lax.psum(jnp.sum(normed_grad * normed, axis=1), "head")
    output = (normed * gain).astype(jnp.bfloat16)
    gain_part = jnp.sum(grad_wide * normed, axis=0)
    flat_grad = (normed_grad - normed * (projected / total_channels)[:, None]) * inverse[:, None]
    attended_grad = to_blocks(flat_grad, heads_local, block_count, block_rows)
    score_grad = (
        jnp.einsum("hnid,hnjd->hnij", attended_grad, value_blocks, precision=highest) * mask_decay
    )
    query_grad = jnp.einsum("hnij,hnjd->hnid", score_grad, key_blocks, precision=highest)
    query_grad = query_grad + from_start * jnp.einsum(
        "hnie,hnde->hnid", attended_grad, entering, precision=highest
    )
    key_grad = jnp.einsum("hnij,hnid->hnjd", score_grad, query_blocks, precision=highest)
    value_grad = jnp.einsum("hnij,hnid->hnjd", scores, attended_grad, precision=highest)
    own_back = jnp.einsum(
        "hnid,hnie->hnde", query_blocks * from_start, attended_grad, precision=highest
    )
    device_back = jnp.zeros_like(device_state)
    for block_index in reversed(range(block_count)):
        device_back = (
            own_back[:, block_index]
            + jnp.exp(block_total[:, block_index])[:, None, None] * device_back
        )
    later_sum = carry_backward(device_decay, device_back)
    leaving = []
    running = later_sum
    for block_index in reversed(range(block_count)):
        leaving.append(running)
        running = (
            own_back[:, block_index] + jnp.exp(block_total[:, block_index])[:, None, None] * running
        )
    leaving = jnp.stack(leaving[::-1], axis=1)
    key_grad = key_grad + to_end * jnp.einsum(
        "hnje,hnde->hnjd", value_blocks, leaving, precision=highest
    )
    value_grad = value_grad + to_end * jnp.einsum(
        "hnjd,hnde->hnje", key_blocks, leaving, precision=highest
    )
    gain_grad = lax.psum(gain_part, "seq")
    return (
        output,
        from_blocks(query_grad).astype(jnp.bfloat16),
        from_blocks(key_grad).astype(jnp.bfloat16),
        from_blocks(value_grad).astype(jnp.bfloat16),
        gain_grad,
    )


def solution(mesh):
    in_specs = (
        P("seq", "head"),
        P("seq", "head"),
        P("seq", "head"),
        P("head", "seq"),
        P("head"),
        P("seq", "head"),
    )
    out_specs = (P("seq", "head"), P("seq", "head"), P("seq", "head"), P("seq", "head"), P("head"))
    return jax.shard_map(local, mesh=mesh, in_specs=in_specs, out_specs=out_specs, check_vma=False)
```

profile of v0, /device:TPU:0, one launch (start us, length us, event | category | flops | bytes accessed | tf_op | source)
XLA Modules:
  0.0 285.3 jit_solution(13174040244083636532)
XLA Ops:
  1.4 2.3 reduce-window.6
  4.4 3.7 %copy.151 = bf16[128,8,8,128]{3,2,1,0:T(8,128)(2,1)} copy(bf16[128,8,8,128]{3,1,2,0:T(8,128)(2,1)} %bitcast.256) | data formatting | bytes 4194304
  8.7 1.5 bitcast_bitcast_fusion.1
  10.2 4.3 %copy.82 = bf16[4,256,8,128]{1,3,0,2:T(8,128)(2,1)} copy(bf16[4,256,8,128]{3,2,1,0:T(8,128)(2,1)} %bitcast.247) | data formatting | bytes 4194304 | tf_op jit(solution)/shard_map/reshape | solution.py:18
  14.5 3.0 %bitcast_bitcast_fusion.2 = bf16[8,4,256,128]{3,0,2,1:T(8,128)(2,1)} fusion(bf16[4,256,8,128]{3,2,1,0:T(8,128)(2,1)} %bitcast.248), kind=kLoop, calls=%fused_computation.124 | loop fusion | bytes 4194304 | tf_op jit(solution)/shard_map/transpose | solution.py:18
  17.5 4.3 %copy.120 = bf16[8,4,256,128]{2,3,1,0:T(8,128)(2,1)} copy(bf16[8,4,256,128]{3,0,2,1:T(8,128)(2,1)} %bitcast_bitcast_fusion.2) | data formatting | bytes 4194304 | tf_op jit(solution)/shard_map/transpose | solution.py:18
  21.8 2.2 copy.152
  24.0 5.6 %fusion.31 = f32[8,4,128,128]{3,2,1,0:T(8,128)S(1)} fusion(f32[8,4,256]{2,1,0:T(4,128)S(1)} %copy.92, bf16[4,256,8,128]{3,2,1,0:T(8,128)(2,1)S(1)} %bitcast.238, bf16[4,256,8,128]{3,2,1,0:T(8,128)(2,1)S(1)} %bitcast.243), kind=kOutput, calls=%fused_computation.40 | convolution fusion | flops 1612709888 | bytes 6324224 | tf_op jit(solution)/shard_map/hnjd,hnje->hnde/dot_general | solution.py:68
  31.1 48.3 %while.24 = (s32[]{:T(128)}, f32[8,128,128]{2,1,0:T(8,128)S(1)}, f32[8,1,1]{0,2,1:T(1,128)S(1)}, f32[8,128,128]{2,1,0:T(8,128)S(1)}, s32[]{:T(128)}) while((s32[]{:T(128)}, f32[8,128,128]{2,1,0:T(8,128)S(1)}, f32[8,1,1]{0,2,1:T(1,128)S(1)}, f32[8,128,128]{2,1,0:T(8,128)S(1)}, s32[]{:T(128)}) %tuple.64), condition=%wide.region_4.5_spmd, body=%wide.region_3.4_spmd.sunk | while | flops 262146 | bytes 3670149 | solution.py:32
  32.0 4.9 %collective-permute-start = (f32[8,128,128]{2,1,0:T(8,128)}, f32[8,128,128]{2,1,0:T(8,128)S(1)}, u32[]{:S(2)}, u32[]{:S(2)}) collective-permute-start(f32[8,128,128]{2,1,0:T(8,128)} %multiply_add_fusion.10), channel_id=1, source_target_pairs={{0,8},{8,16},{16,24},{1,9},{9,17},{17,25},{2,10},{10,18},{18,26},{... | collective-permute-start | bytes 1572872 | tf_op jit(solution)/shard_map/while/body/eval_jaxpr/ppermute | solution.py:13
  36.9 11.4 %collective-permute-done = f32[8,128,128]{2,1,0:T(8,128)S(1)} collective-permute-done((f32[8,128,128]{2,1,0:T(8,128)}, f32[8,128,128]{2,1,0:T(8,128)S(1)}, u32[]{:S(2)}, u32[]{:S(2)}) %collective-permute-start) | collective-permute-done | bytes 524320 | tf_op jit(solution)/shard_map/while/body/eval_jaxpr/ppermute | solution.py:13
  49.3 4.3 %collective-permute-start = (f32[8,128,128]{2,1,0:T(8,128)}, f32[8,128,128]{2,1,0:T(8,128)S(1)}, u32[]{:S(2)}, u32[]{:S(2)}) collective-permute-start(f32[8,128,128]{2,1,0:T(8,128)} %multiply_add_fusion.10), channel_id=1, source_target_pairs={{0,8},{8,16},{16,24},{1,9},{9,17},{17,25},{2,10},{10,18},{18,26},{... | collective-permute-start | bytes 1572872 | tf_op jit(solution)/shard_map/while/body/eval_jaxpr/ppermute | solution.py:13
  53.6 10.6 %collective-permute-done = f32[8,128,128]{2,1,0:T(8,128)S(1)} collective-permute-done((f32[8,128,128]{2,1,0:T(8,128)}, f32[8,128,128]{2,1,0:T(8,128)S(1)}, u32[]{:S(2)}, u32[]{:S(2)}) %collective-permute-start) | collective-permute-done | bytes 524320 | tf_op jit(solution)/shard_map/while/body/eval_jaxpr/ppermute | solution.py:13
  65.1 4.3 %collective-permute-start = (f32[8,128,128]{2,1,0:T(8,128)}, f32[8,128,128]{2,1,0:T(8,128)S(1)}, u32[]{:S(2)}, u32[]{:S(2)}) collective-permute-start(f32[8,128,128]{2,1,0:T(8,128)} %multiply_add_fusion.10), channel_id=1, source_target_pairs={{0,8},{8,16},{16,24},{1,9},{9,17},{17,25},{2,10},{10,18},{18,26},{... | collective-permute-start | bytes 1572872 | tf_op jit(solution)/shard_map/while/body/eval_jaxpr/ppermute | solution.py:13
  69.4 9.7 %collective-permute-done = f32[8,128,128]{2,1,0:T(8,128)S(1)} collective-permute-done((f32[8,128,128]{2,1,0:T(8,128)}, f32[8,128,128]{2,1,0:T(8,128)S(1)}, u32[]{:S(2)}, u32[]{:S(2)}) %collective-permute-start) | collective-permute-done | bytes 524320 | tf_op jit(solution)/shard_map/while/body/eval_jaxpr/ppermute | solution.py:13
  79.4 1.7 add_bitcast_fusion.1
  81.4 3.2 %fusion.60 = f32[8,4,256,256]{3,2,1,0:T(8,128)S(1)} fusion(bf16[8,4,256,128]{2,3,1,0:T(8,128)(2,1)S(1)} %copy-done.3, bf16[4,256,8,128]{3,2,1,0:T(8,128)(2,1)} %bitcast.244), kind=kOutput, calls=%fused_computation.74 | convolution fusion | flops 536870912 | bytes 12582912 | tf_op jit(solution)/shard_map/hnid,hnjd->hnij/dot_general | solution.py:64
  84.6 7.0 %fusion.4 = f32[8,4,256,128]{2,3,1,0:T(8,128)S(1)} fusion(f32[8,4,256,256]{3,2,1,0:T(8,128)S(1)} %fusion.60, f32[8,4,256]{2,1,0:T(4,128)S(1)} %copy.87, pred[256,256]{1,0:T(8,128)(4,1)S(1)} %iota_compare_fusion, bf16[8,4,256,128]{3,0,2,1:T(8,128)(2,1)S(1)} %copy-done.25), kind=kOutput, calls=%fused_computation.6 | convolution fusion | flops 3227516928 | bytes 14778368 | tf_op jit(solution)/shard_map/hnij,hnjd->hnid/dot_general | solution.py:67
  91.6 4.7 %multiply_reduce_fusion = (f32[4,256]{1,0:T(4,128)S(1)}, f32[4,256,8,128]{1,3,0,2:T(8,128)}) fusion(bf16[8,4,256,128]{2,3,1,0:T(8,128)(2,1)S(1)} %copy-done.3, f32[4,256,8]{1,0,2:T(4,128)S(1)} %copy.91, f32[8,4,256,128]{2,3,1,0:T(8,128)S(1)} %fusion.4, f32[8,1,128,128]{3,2,0,1:T(8,128)S(1)} %get-tuple-element.129, f32[8,1,128,128]{3,2,0,1:T(8,128)S(1)} %bitcast.252, ...), kind=kOutput, calls=%fused_computation.39 | convolution fusion | flops 1616378880 | bytes 12619776 | tf_op jit(solution)/shard_map/hnid,hnde->hnie/dot_general | solution.py:86
  96.3 11.8 %psum.21 = f32[1024]{0:T(1024)S(1)} all-reduce(f32[1024]{0:T(1024)S(1)} %bitcast.265), channel_id=1, replica_groups=mesh['seq'=4,'head'=8] {'head'}, use_global_device_ids=true, to_apply=%region_6.7 | all-reduce | flops 1024 | bytes 8192 | tf_op jit(solution)/shard_map/psum | solution.py:92
  108.2 5.8 %copy.99 = f32[4,256,8,128]{3,2,1,0:T(8,128)} copy(f32[4,256,8,128]{1,3,0,2:T(8,128)} %get-tuple-element.145) | data formatting | bytes 8388608 | tf_op jit(solution)/shard_map/add | solution.py:86
  114.0 4.5 %fusion.15 = (f32[1024]{0:T(1024)S(1)}, f32[1024]{0:T(1024)S(1)}) fusion(bf16[1024,1024]{1,0:T(8,128)(2,1)} %param.15, f32[128,8,8,128]{3,2,1,0:T(8,128)} %bitcast.241, f32[1024]{0:T(1024)S(1)} %add_rsqrt_fusion, f32[1024]{0:T(1024)S(1)} %copy-done.26), kind=kLoop, calls=%fused_computation.16 | loop fusion | flops 7337984 | bytes 6307840 | tf_op jit(solution)/shard_map/reduce_sum | solution.py:97
  118.5 13.4 %psum.23 = f32[1024]{0:T(1024)} all-reduce(f32[1024]{0:T(1024)S(1)} %get-tuple-element.107), channel_id=1, replica_groups=mesh['seq'=4,'head'=8] {'seq'}, use_global_device_ids=true, to_apply=%region_12.13 | all-reduce | flops 1024 | bytes 8192 | tf_op jit(solution)/shard_map/psum | solution.py:133
  131.8 11.8 %psum.22 = f32[1024]{0:T(1024)S(1)} all-reduce(f32[1024]{0:T(1024)S(1)} %get-tuple-element.108), channel_id=1, replica_groups=mesh['seq'=4,'head'=8] {'head'}, use_global_device_ids=true, to_apply=%region_8.9 | all-reduce | flops 1024 | bytes 8192 | tf_op jit(solution)/shard_map/psum | solution.py:95
  143.6 5.1 %fusion.14 = (f32[128,8,8,128]{3,1,2,0:T(8,128)S(1)}, bf16[1024,1024]{1,0:T(8,128)(2,1)}) fusion(bf16[1024,1024]{1,0:T(8,128)(2,1)} %param.15, f32[128,8,8,128]{3,2,1,0:T(8,128)} %bitcast.242, f32[1024]{0:T(1024)S(1)} %broadcast_multiply_fusion, f32[1024]{0:T(1024)S(1)} %copy-done.26, f32[1024]{0:T(1024)S(1)} %add_rsqrt_fusion), kind=kLoop, calls=%fused_computation.15 | loop fusion | flops 8388608 | bytes 12595200
  149.7 20.4 %fusion.2 = f32[8,4,256,128]{3,2,1,0:T(8,128)} fusion(f32[8,4,256,256]{3,2,1,0:T(8,128)} %copy-done.2, f32[8,4,256]{2,1,0:T(4,128)S(1)} %copy.87, pred[256,256]{1,0:T(8,128)(4,1)S(1)} %iota_compare_fusion, f32[4,256,8,128]{3,2,1,0:T(8,128)S(1)} %bitcast.229), kind=kOutput, calls=%fused_computation.5 | convolution fusion | flops 3227516928 | bytes 16875520 | tf_op jit(solution)/shard_map/hnij,hnid->hnjd/dot_general | solution.py:108
  170.4 1.3 copy-done.8
  171.7 5.3 %fusion.20 = f32[8,4,128,128]{3,2,0,1:T(8,128)S(1)} fusion(f32[8,4,256,128]{3,0,2,1:T(8,128)S(1)} %bitcast_bitcast_fusion, bf16[4,256,8,128]{1,3,0,2:T(8,128)(2,1)S(1)} %copy-done.8, f32[8,4,256]{2,1,0:T(4,128)S(1)} %copy.108), kind=kOutput, calls=%fused_computation.24 | convolution fusion | flops 1612709888 | bytes 8421376 | tf_op jit(solution)/shard_map/hnid,hnie->hnde/dot_general | solution.py:109
  177.1 1.3 copy-done.7
  179.5 50.6 %while.25 = (s32[]{:T(128)}, f32[8,128,128]{2,1,0:T(8,128)S(1)}, f32[8,1,1]{0,2,1:T(1,128)S(1)}, f32[8,128,128]{2,1,0:T(8,128)}, s32[]{:T(128)}) while((s32[]{:T(128)}, f32[8,128,128]{2,1,0:T(8,128)S(1)}, f32[8,1,1]{0,2,1:T(1,128)S(1)}, f32[8,128,128]{2,1,0:T(8,128)}, s32[]{:T(128)}) %tuple.70), condition=%wide.region_10.11_spmd, body=%wide.region_9.10_spmd.sunk | while | flops 262146 | bytes 3670149 | solution.py:41
  179.5 2.0 multiply_add_fusion.11
  182.7 14.5 %collective-permute-done.1 = f32[8,128,128]{2,1,0:T(8,128)S(1)} collective-permute-done((f32[8,128,128]{2,1,0:T(8,128)}, f32[8,128,128]{2,1,0:T(8,128)S(1)}, u32[]{:S(2)}, u32[]{:S(2)}) %collective-permute-start.1) | collective-permute-done | bytes 524320 | tf_op jit(solution)/shard_map/while/body/eval_jaxpr/ppermute | solution.py:13
  197.2 2.0 multiply_add_fusion.11
  200.5 13.6 %collective-permute-done.1 = f32[8,128,128]{2,1,0:T(8,128)S(1)} collective-permute-done((f32[8,128,128]{2,1,0:T(8,128)}, f32[8,128,128]{2,1,0:T(8,128)S(1)}, u32[]{:S(2)}, u32[]{:S(2)}) %collective-permute-start.1) | collective-permute-done | bytes 524320 | tf_op jit(solution)/shard_map/while/body/eval_jaxpr/ppermute | solution.py:13
  214.1 2.0 multiply_add_fusion.11
  217.3 12.7 %collective-permute-done.1 = f32[8,128,128]{2,1,0:T(8,128)S(1)} collective-permute-done((f32[8,128,128]{2,1,0:T(8,128)}, f32[8,128,128]{2,1,0:T(8,128)S(1)}, u32[]{:S(2)}, u32[]{:S(2)}) %collective-permute-start.1) | collective-permute-done | bytes 524320 | tf_op jit(solution)/shard_map/while/body/eval_jaxpr/ppermute | solution.py:13
  230.1 1.7 add_bitcast_fusion
  232.1 4.9 %fusion.17 = bf16[4,256,8,128]{3,1,0,2:T(8,128)(2,1)S(1)} fusion(f32[8,4,256,128]{3,2,1,0:T(8,128)} %fusion.2, f32[4,256,8]{1,0,2:T(4,128)S(1)} %copy.107, bf16[4,256,8,128]{3,2,1,0:T(8,128)(2,1)S(1)} %bitcast.246, f32[8,1,128,128]{3,2,0,1:T(8,128)S(1)} %bitcast.233, f32[8,1,128,128]{3,2,0,1:T(8,128)S(1)} %get-tuple-element.133, ...), kind=kOutput, calls=%fused_computation.20 | convolution fusion | flops 1615331328 | bytes 10518528 | tf_op jit(solution)/shard_map/hnjd,hnde->hnje/dot_general | solution.py:130
  237.1 2.7 copy.119
  239.8 4.1 %fusion.27 = f32[8,4,256,256]{3,2,1,0:T(8,128)S(1)} fusion(f32[4,256,8,128]{3,2,1,0:T(8,128)S(1)} %bitcast.231, bf16[4,256,8,128]{3,2,1,0:T(8,128)(2,1)S(1)} %bitcast.239), kind=kOutput, calls=%fused_computation.32 | convolution fusion | flops 3221225472 | bytes 14680064 | tf_op jit(solution)/shard_map/hnid,hnjd->hnij/dot_general | solution.py:101
  243.9 11.2 %fusion.6 = f32[8,4,256,128]{3,2,1,0:T(8,128)} fusion(bf16[8,4,256,128]{2,3,1,0:T(8,128)(2,1)} %copy.120, f32[8,4,256,256]{3,2,1,0:T(8,128)S(1)} %fusion.27, f32[8,4,256]{2,1,0:T(4,128)S(1)} %copy.87, pred[256,256]{1,0:T(8,128)(4,1)S(1)} %iota_compare_fusion), kind=kOutput, calls=%fused_computation.7 | convolution fusion | flops 3227516928 | bytes 14778368 | tf_op jit(solution)/shard_map/hnij,hnid->hnjd/dot_general | solution.py:107
  255.0 8.9 %fusion.8 = f32[8,4,256,128]{2,3,1,0:T(8,128)S(1)} fusion(f32[8,4,256,256]{3,2,1,0:T(8,128)S(1)} %fusion.27, f32[8,4,256]{2,1,0:T(4,128)S(1)} %copy.87, pred[256,256]{1,0:T(8,128)(4,1)S(1)} %iota_compare_fusion, bf16[4,256,8,128]{3,2,1,0:T(8,128)(2,1)} %bitcast.245), kind=kOutput, calls=%fused_computation.8 | convolution fusion | flops 3227516928 | bytes 14778368 | tf_op jit(solution)/shard_map/hnij,hnjd->hnid/dot_general | solution.py:103
  264.0 6.0 %fusion.23 = bf16[4,256,8,128]{1,3,0,2:T(8,128)(2,1)} fusion(f32[8,4,256,128]{2,3,1,0:T(8,128)S(1)} %fusion.8, f32[4,256,8]{1,0,2:T(4,128)S(1)} %copy.91, f32[4,256,8,128]{3,2,1,0:T(8,128)S(1)} %bitcast.232, f32[8,1,128,128]{3,2,0,1:T(8,128)S(1)} %copy-done.13, f32[8,1,128,128]{3,2,0,1:T(8,128)S(1)} %bitcast.253, f32[8,1,128,128]{3,2,0,1:T(8,128)S(1)} %copy-done.17, ...), kind=kOutput, calls=%fused_computation.28 | convolution fusion | flops 1615331328 | bytes 12615680 | tf_op jit(solution)/shard_map/hnie,hnde->hnid/dot_general | solution.py:104
  270.0 2.9 %fusion.19 = bf16[4,256,8,128]{3,1,0,2:T(8,128)(2,1)S(1)} fusion(f32[8,4,256,128]{3,2,1,0:T(8,128)S(1)} %copy-done.6, f32[4,256,8]{1,0,2:T(4,128)S(1)} %copy.107, bf16[4,256,8,128]{3,2,1,0:T(8,128)(2,1)S(1)} %bitcast.240, f32[8,1,128,128]{3,2,0,1:T(8,128)S(1)} %bitcast.234, f32[8,1,128,128]{3,2,0,1:T(8,128)S(1)} %copy-done.23, ...), kind=kOutput, calls=%fused_computation.23 | convolution fusion | flops 1615331328 | bytes 10518528 | tf_op jit(solution)/shard_map/hnje,hnde->hnjd/dot_general | solution.py:127
  272.9 2.7 copy.115
  275.6 3.1 %copy.104 = bf16[4,256,8,128]{3,2,1,0:T(8,128)(2,1)S(1)} copy(bf16[4,256,8,128]{1,3,0,2:T(8,128)(2,1)} %fusion.23) | data formatting | bytes 4194304 | tf_op jit(solution)/shard_map/convert_element_type | solution.py:136
  278.7 2.0 copy.239
  281.7 3.3 %copy_bitcast_fusion = (bf16[1024,1024]{1,0:T(8,128)(2,1)}, bf16[1024,1024]{1,0:T(8,128)(2,1)}) fusion(bf16[128,8,8,128]{3,2,1,0:T(8,128)(2,1)S(1)} %bitcast.250, bf16[128,8,8,128]{3,2,1,0:T(8,128)(2,1)S(1)} %bitcast.251), kind=kLoop, calls=%fused_computation.62 | loop fusion | bytes 8388608 | tf_op jit(solution)/shard_map/convert_element_type | solution.py:138
  (84 shorter events, 14.1 us)
Async XLA Ops:
  4.4 3.7 %copy-start.24 = (bf16[1024,1024]{1,0:T(8,128)(2,1)S(1)}, bf16[1024,1024]{1,0:T(8,128)(2,1)}, u32[]{:S(2)}) copy-start(bf16[1024,1024]{1,0:T(8,128)(2,1)} %param.12) | copy-start | bytes 6291460
  24.0 5.7 %copy-start.4 = (bf16[128,8,8,128]{3,2,1,0:T(8,128)(2,1)}, bf16[128,8,8,128]{3,2,1,0:T(8,128)(2,1)S(1)}, u32[]{:S(2)}) copy-start(bf16[128,8,8,128]{3,2,1,0:T(8,128)(2,1)S(1)} %copy.152) | copy-start | bytes 6291460
  29.7 1.3 copy-start.11
  32.0 16.4 %collective-permute-start = (f32[8,128,128]{2,1,0:T(8,128)}, f32[8,128,128]{2,1,0:T(8,128)S(1)}, u32[]{:S(2)}, u32[]{:S(2)}) collective-permute-start(f32[8,128,128]{2,1,0:T(8,128)} %multiply_add_fusion.10), channel_id=1, source_target_pairs={{0,8},{8,16},{16,24},{1,9},{9,17},{17,25},{2,10},{10,18},{18,26},{... | collective-permute-start | bytes 1572872 | tf_op jit(solution)/shard_map/while/body/eval_jaxpr/ppermute | solution.py:13
  49.3 14.9 %collective-permute-start = (f32[8,128,128]{2,1,0:T(8,128)}, f32[8,128,128]{2,1,0:T(8,128)S(1)}, u32[]{:S(2)}, u32[]{:S(2)}) collective-permute-start(f32[8,128,128]{2,1,0:T(8,128)} %multiply_add_fusion.10), channel_id=1, source_target_pairs={{0,8},{8,16},{16,24},{1,9},{9,17},{17,25},{2,10},{10,18},{18,26},{... | collective-permute-start | bytes 1572872 | tf_op jit(solution)/shard_map/while/body/eval_jaxpr/ppermute | solution.py:13
  65.1 14.0 %collective-permute-start = (f32[8,128,128]{2,1,0:T(8,128)}, f32[8,128,128]{2,1,0:T(8,128)S(1)}, u32[]{:S(2)}, u32[]{:S(2)}) collective-permute-start(f32[8,128,128]{2,1,0:T(8,128)} %multiply_add_fusion.10), channel_id=1, source_target_pairs={{0,8},{8,16},{16,24},{1,9},{9,17},{17,25},{2,10},{10,18},{18,26},{... | collective-permute-start | bytes 1572872 | tf_op jit(solution)/shard_map/while/body/eval_jaxpr/ppermute | solution.py:13
  79.4 2.1 copy-start.3
  81.1 10.5 %copy-start.12 = (f32[8,1,128,128]{3,2,0,1:T(8,128)}, f32[8,1,128,128]{3,2,0,1:T(8,128)S(1)}, u32[]{:S(2)}) copy-start(f32[8,1,128,128]{3,2,0,1:T(8,128)S(1)} %get-tuple-element.129) | copy-start | bytes 1572868
  81.1 10.5 %copy-start.14 = (f32[8,128,128]{2,1,0:T(8,128)}, f32[8,128,128]{2,1,0:T(8,128)S(1)}, u32[]{:S(2)}) copy-start(f32[8,128,128]{2,1,0:T(8,128)S(1)} %get-tuple-element.130) | copy-start | bytes 1572868
  81.1 10.5 %copy-start.16 = (f32[8,1,128,128]{3,2,0,1:T(8,128)}, f32[8,1,128,128]{3,2,0,1:T(8,128)S(1)}, u32[]{:S(2)}) copy-start(f32[8,1,128,128]{3,2,0,1:T(8,128)S(1)} %get-tuple-element.134) | copy-start | bytes 1572868
  81.4 3.2 %copy-start.25 = (bf16[8,4,256,128]{3,0,2,1:T(8,128)(2,1)S(1)}, bf16[8,4,256,128]{3,0,2,1:T(8,128)(2,1)}, u32[]{:S(2)}) copy-start(bf16[8,4,256,128]{3,0,2,1:T(8,128)(2,1)} %bitcast_bitcast_fusion.1) | copy-start | bytes 6291460
  84.6 7.0 %copy-start.2 = (f32[8,4,256,256]{3,2,1,0:T(8,128)}, f32[8,4,256,256]{3,2,1,0:T(8,128)S(1)}, u32[]{:S(2)}) copy-start(f32[8,4,256,256]{3,2,1,0:T(8,128)S(1)} %fusion.60) | copy-start | bytes 25165828
  108.2 5.8 %copy-start.26 = (f32[1024]{0:T(1024)S(1)}, f32[1024]{0:T(1024)}, u32[]{:S(2)}) copy-start(f32[1024]{0:T(1024)} %param.14) | copy-start | bytes 12292
  149.7 20.4 %copy-start = (f32[128,8,8,128]{3,2,1,0:T(8,128)}, f32[128,8,8,128]{3,2,1,0:T(8,128)S(1)}, u32[]{:S(2)}) copy-start(f32[128,8,8,128]{3,2,1,0:T(8,128)S(1)} %copy.156) | copy-start | bytes 12582916
  170.1 1.6 copy-start.8
  177.1 1.3 copy-start.7
  181.4 15.8 %collective-permute-start.1 = (f32[8,128,128]{2,1,0:T(8,128)}, f32[8,128,128]{2,1,0:T(8,128)S(1)}, u32[]{:S(2)}, u32[]{:S(2)}) collective-permute-start(f32[8,128,128]{2,1,0:T(8,128)} %multiply_add_fusion.11), channel_id=1, source_target_pairs={{8,0},{16,8},{24,16},{9,1},{17,9},{25,17},{10,2},{18,10},{26,18},{... | collective-permute-start | bytes 1572872 | tf_op jit(solution)/shard_map/while/body/eval_jaxpr/ppermute | solution.py:13
  199.2 14.9 %collective-permute-start.1 = (f32[8,128,128]{2,1,0:T(8,128)}, f32[8,128,128]{2,1,0:T(8,128)S(1)}, u32[]{:S(2)}, u32[]{:S(2)}) collective-permute-start(f32[8,128,128]{2,1,0:T(8,128)} %multiply_add_fusion.11), channel_id=1, source_target_pairs={{8,0},{16,8},{24,16},{9,1},{17,9},{25,17},{10,2},{18,10},{26,18},{... | collective-permute-start | bytes 1572872 | tf_op jit(solution)/shard_map/while/body/eval_jaxpr/ppermute | solution.py:13
  216.1 14.0 %collective-permute-start.1 = (f32[8,128,128]{2,1,0:T(8,128)}, f32[8,128,128]{2,1,0:T(8,128)S(1)}, u32[]{:S(2)}, u32[]{:S(2)}) collective-permute-start(f32[8,128,128]{2,1,0:T(8,128)} %multiply_add_fusion.11), channel_id=1, source_target_pairs={{8,0},{16,8},{24,16},{9,1},{17,9},{25,17},{10,2},{18,10},{26,18},{... | collective-permute-start | bytes 1572872 | tf_op jit(solution)/shard_map/while/body/eval_jaxpr/ppermute | solution.py:13
  230.0 2.1 copy-start.5
  231.8 5.3 %copy-start.18 = (f32[8,1,128,128]{3,2,0,1:T(8,128)}, f32[8,1,128,128]{3,2,0,1:T(8,128)S(1)}, u32[]{:S(2)}) copy-start(f32[8,1,128,128]{3,2,0,1:T(8,128)S(1)} %get-tuple-element.127) | copy-start | bytes 1572868
  231.8 5.3 %copy-start.20 = (f32[8,128,128]{2,1,0:T(8,128)}, f32[8,128,128]{2,1,0:T(8,128)S(1)}, u32[]{:S(2)}) copy-start(f32[8,128,128]{2,1,0:T(8,128)S(1)} %get-tuple-element.128) | copy-start | bytes 1572868
  231.8 5.3 %copy-start.22 = (f32[8,1,128,128]{3,2,0,1:T(8,128)}, f32[8,1,128,128]{3,2,0,1:T(8,128)S(1)}, u32[]{:S(2)}) copy-start(f32[8,1,128,128]{3,2,0,1:T(8,128)S(1)} %get-tuple-element.133) | copy-start | bytes 1572868
  237.1 2.7 copy-start.1
  255.0 8.9 %copy-start.13 = (f32[8,1,128,128]{3,2,0,1:T(8,128)S(1)}, f32[8,1,128,128]{3,2,0,1:T(8,128)}, u32[]{:S(2)}) copy-start(f32[8,1,128,128]{3,2,0,1:T(8,128)} %copy-done.12) | copy-start | bytes 1572868
  255.0 8.9 %copy-start.15 = (f32[8,128,128]{2,1,0:T(8,128)S(1)}, f32[8,128,128]{2,1,0:T(8,128)}, u32[]{:S(2)}) copy-start(f32[8,128,128]{2,1,0:T(8,128)} %copy-done.14) | copy-start | bytes 1572868
  255.0 8.9 %copy-start.17 = (f32[8,1,128,128]{3,2,0,1:T(8,128)S(1)}, f32[8,1,128,128]{3,2,0,1:T(8,128)}, u32[]{:S(2)}) copy-start(f32[8,1,128,128]{3,2,0,1:T(8,128)} %copy-done.16) | copy-start | bytes 1572868
  264.0 6.0 %copy-start.6 = (f32[8,4,256,128]{3,2,1,0:T(8,128)S(1)}, f32[8,4,256,128]{3,2,1,0:T(8,128)}, u32[]{:S(2)}) copy-start(f32[8,4,256,128]{3,2,1,0:T(8,128)} %fusion.6) | copy-start | bytes 12582916
  264.0 6.0 %copy-start.19 = (f32[8,1,128,128]{3,2,0,1:T(8,128)S(1)}, f32[8,1,128,128]{3,2,0,1:T(8,128)}, u32[]{:S(2)}) copy-start(f32[8,1,128,128]{3,2,0,1:T(8,128)} %copy-done.18) | copy-start | bytes 1572868
  264.0 6.0 %copy-start.21 = (f32[8,128,128]{2,1,0:T(8,128)S(1)}, f32[8,128,128]{2,1,0:T(8,128)}, u32[]{:S(2)}) copy-start(f32[8,128,128]{2,1,0:T(8,128)} %copy-done.20) | copy-start | bytes 1572868
  264.0 6.0 %copy-start.23 = (f32[8,1,128,128]{3,2,0,1:T(8,128)S(1)}, f32[8,1,128,128]{3,2,0,1:T(8,128)}, u32[]{:S(2)}) copy-start(f32[8,1,128,128]{3,2,0,1:T(8,128)} %copy-done.22) | copy-start | bytes 1572868
  278.7 2.0 copy-start.9
  278.7 3.0 %copy-start.10 = (bf16[4,256,8,128]{3,2,1,0:T(8,128)(2,1)S(1)}, bf16[4,256,8,128]{3,2,1,0:T(8,128)(2,1)}, u32[]{:S(2)}) copy-start(bf16[4,256,8,128]{3,2,1,0:T(8,128)(2,1)} %copy.115) | copy-start | bytes 6291460
where the time goes:
time: 290 us; the launch traced here: 285 us
  matrix products  84.1 us (29%)
  waiting for transfers between devices  72.5 us (25%)
  local copies, waits for them, and re-layouts  46.9 us (16%)
  blocking collectives  37 us (13%)
  other arithmetic  25.6 us (9%)
  starting transfers between devices  17.4 us (6%)
    ppermute x6, waiting for transfers between devices, passed_along(): lax.ppermute(value, axis, [(source, source + steps) for source in range(i...  72.5 us
    dot_general x1, matrix products, local(): jnp.einsum('hnij,hnid->hnjd', scores, attended_grad, precision=highest)  20.4 us
    ppermute x6, starting transfers between devices, passed_along(): lax.ppermute(value, axis, [(source, source + steps) for source in range(i...  17.4 us
    unnamed x60, local copies, waits for them, and re-layouts  14.9 us
    psum x1, blocking collectives, local(): gain_grad = lax.psum(gain_part, 'seq')  13.4 us
    psum x1, blocking collectives, local(): squares = lax.psum(jnp.sum(flattened * flattened, axis=1), 'head')  11.8 us
    psum x1, blocking collectives, local(): projected = lax.psum(jnp.sum(normed_grad * normed, axis=1), 'head')  11.8 us
    dot_general x1, matrix products, local(): jnp.einsum('hnij,hnid->hnjd', score_grad, query_blocks, precision=highest)  11.2 us
  transfers between devices with their start and end apart: 6, of which 6 were waited for; matrix products, arithmetic and copies ran while one was open for 0% of the time, Pallas kernels for 0%

commit v1 on v0

v1 whole, which is shorter than its diff:
```python
import functools

import jax
import jax.numpy as jnp
from jax import lax
from jax.experimental import pallas as pl
from jax.experimental.pallas import tpu as pltpu
from jax.sharding import PartitionSpec as P

epsilon = 1e-06
highest = lax.Precision.HIGHEST
MESH = pl.DeviceIdType.MESH
WIDTH = 128
f32, bf16 = jnp.float32, jnp.bfloat16


def dot(a, b, ca=1, cb=0):
    return lax.dot_general(a, b, (((ca,), (cb,)), ((), ())), preferred_element_type=f32)


def split(x):
    high = x.astype(bf16)
    return high, (x - high.astype(f32)).astype(bf16)


def kernel(
    seq_count, head_count, heads, rows,
    decay, gain, q_hbm, k_hbm, v_hbm, g_hbm,
    out_hbm, dq_hbm, dk_hbm, dv_hbm, dgain,
    q, k, v, g, out, dq, dk, dv,
    attn, sums_g, cols_g, own, entering, back, mask, p_high, p_low,
    f_in, f_out, b_in, b_out, acc_sq, acc_pr, norm, alpha, beta, gparts,
    in_sem, out_sem, f_send, f_recv, b_send, b_recv, n_send, n_recv, g_send, g_recv,
):
    z = lax.axis_index("seq")
    me = lax.axis_index("head")
    size = min(256, rows)
    count = rows // size
    channels = heads * WIDTH * head_count

    def cols(h):
        return pl.ds(pl.multiple_of(h * WIDTH, WIDTH), WIDTH)

    def load(n, h):
        hbm, ref = ((k_hbm, k), (v_hbm, v), (q_hbm, q), (g_hbm, g))[n]
        return pltpu.make_async_copy(hbm.at[:, cols(h)], ref.at[:, cols(h)], in_sem.at[n, h])

    def store(n, h):
        hbm, ref = ((out_hbm, out), (dq_hbm, dq), (dk_hbm, dk), (dv_hbm, dv))[n]
        return pltpu.make_async_copy(ref.at[:, cols(h)], hbm.at[:, cols(h)], out_sem.at[n, h])

    def forward(h):
        return pltpu.make_async_remote_copy(
            src_ref=f_out.at[h], dst_ref=f_in.at[h], send_sem=f_send.at[h], recv_sem=f_recv.at[h],
            device_id=(lax.rem(z + 1, seq_count), me), device_id_type=MESH)

    def backward(h):
        return pltpu.make_async_remote_copy(
            src_ref=b_out.at[h], dst_ref=b_in.at[h], send_sem=b_send.at[h], recv_sem=b_recv.at[h],
            device_id=(lax.rem(z + seq_count - 1, seq_count), me), device_id_type=MESH)

    for h in range(heads):
        load(0, h).start()
        load(1, h).start()
    for h in range(heads):
        load(2, h).start()
        load(3, h).start()

    barrier = pltpu.get_barrier_semaphore()
    for step in range(1, head_count):
        pl.semaphore_signal(barrier, inc=1, device_id=(z, lax.rem(me + step, head_count)), device_id_type=MESH)
    for step in range(1, seq_count):
        pl.semaphore_signal(barrier, inc=1, device_id=(lax.rem(z + step, seq_count), me), device_id_type=MESH)

    below = lax.broadcasted_iota(jnp.int32, (size, size), 0) >= lax.broadcasted_iota(jnp.int32, (size, size), 1)
    above = lax.broadcasted_iota(jnp.int32, (size, size), 0) <= lax.broadcasted_iota(jnp.int32, (size, size), 1)
    tri = jnp.where(above, 1.0, 0.0).astype(f32)
    for b in range(count):
        at = pl.ds(b * size, size)
        sums_g[:, at] = jnp.dot(decay[:, at], tri, precision=highest, preferred_element_type=f32)
    acc_sq[...] = jnp.zeros_like(acc_sq)
    acc_pr[...] = jnp.zeros_like(acc_pr)
    pl.semaphore_wait(barrier, head_count - 1 + seq_count - 1)

    def total(h, b):
        return cols_g[(b + 1) * size - 1:(b + 1) * size, cols(h)]

    def states(h, carry):
        load(0, h).wait()
        load(1, h).wait()
        state = jnp.zeros((WIDTH, WIDTH), f32)
        for b in range(count):
            at = pl.ds(b * size, size)
            column = jnp.broadcast_to(sums_g[pl.ds(h, 1), at], (WIDTH, size)).T
            cols_g[at, cols(h)] = column
            last = column[size - 1:size, :]
            high, low = split(v[at, cols(h)].astype(f32) * jnp.exp(last - column))
            both = dot(k[at, cols(h)], jnp.concatenate([high, low], axis=1), 0, 0)
            mine = both[:, :WIDTH] + both[:, WIDTH:]
            own[h, b] = mine
            state = jnp.exp(last) * state + mine
        f_out[h] = state

        @pl.when(z == 0)
        def _():
            f_in[h] = jnp.zeros((WIDTH, WIDTH), f32)
            forward(h).start()
        return carry

    lax.fori_loop(0, heads, states, 0)

    def device_total(h):
        result = total(h, 0)
        for b in range(1, count):
            result = result + total(h, b)
        return result

    def attend(h, carry):
        load(2, h).wait()
        load(3, h).wait()
        for b in range(count):
            at = pl.ds(b * size, size)
            wide = jnp.concatenate([cols_g[at, cols(h)]] * (size // WIDTH), axis=1)
            m = jnp.exp(jnp.where(below, wide - sums_g[pl.ds(h, 1), at], -1e30))
            mask[h, at, :] = m
            high, low = split(dot(q[at, cols(h)], k[at, cols(h)], 1, 1) * m)
            p_high[h, at, :] = high
            p_low[h, at, :] = low
            attn[at, cols(h)] = dot(high, v[at, cols(h)]) + dot(low, v[at, cols(h)])

        @pl.when(z > 0)
        def _():
            forward(h).wait_recv()

            @pl.when(z < seq_count - 1)
            def _():
                f_out[h] = f_out[h] + jnp.exp(device_total(h)) * f_in[h]
                forward(h).start()

        state = f_in[h]
        for b in range(count):
            at = pl.ds(b * size, size)
            entering[h, b] = state
            high, low = split(state)
            query = q[at, cols(h)]
            cross = dot(jnp.concatenate([query, query], axis=1), jnp.concatenate([high, low], axis=0))
            value = attn[at, cols(h)] + jnp.exp(cols_g[at, cols(h)]) * cross
            attn[at, cols(h)] = value
            acc_sq[at, :] = acc_sq[at, :] + value * value
            acc_pr[at, :] = acc_pr[at, :] + value * (g[at, cols(h)].astype(f32) * gain[:, cols(h)])
            state = jnp.exp(total(h, b)) * state + own[h, b]
        return carry

    lax.fori_loop(0, heads, attend, 0)

    for b in range(rows // WIDTH):
        at = pl.ds(b * WIDTH, WIDTH)
        norm[me, 0:1, at] = jnp.sum(acc_sq[at, :].T, axis=0, keepdims=True)
        norm[me, 1:2, at] = jnp.sum(acc_pr[at, :].T, axis=0, keepdims=True)

    def exchange(step):
        return pltpu.make_async_remote_copy(
            src_ref=norm.at[me], dst_ref=norm.at[me], send_sem=n_send.at[step], recv_sem=n_recv.at[step],
            device_id=(z, lax.rem(me + step, head_count)), device_id_type=MESH)

    def arrived(step):
        slot = norm.at[lax.rem(me + head_count - step, head_count)]
        return pltpu.make_async_remote_copy(
            src_ref=slot, dst_ref=slot, send_sem=n_send.at[step], recv_sem=n_recv.at[step],
            device_id=(z, lax.rem(me + step, head_count)), device_id_type=MESH)

    for step in range(1, head_count):
        exchange(step).start()
    for step in range(1, head_count):
        arrived(step).wait_recv()
    summed = norm[0]
    for d in range(1, head_count):
        summed = summed + norm[d]
    inverse = 1.0 / jnp.sqrt(summed[0:1] / channels + epsilon)
    second = inverse * inverse * inverse * (summed[1:2] / channels)
    for b in range(rows // WIDTH):
        at = slice(b * WIDTH, (b + 1) * WIDTH)
        alpha[at, :] = jnp.broadcast_to(inverse[:, at], (WIDTH, WIDTH)).T
        beta[at, :] = jnp.broadcast_to(second[:, at], (WIDTH, WIDTH)).T

    def gradients(h, carry):
        gain_h = gain[:, cols(h)]
        part = jnp.zeros((1, WIDTH), f32)
        state = jnp.zeros((WIDTH, WIDTH), f32)
        for b in reversed(range(count)):
            at = pl.ds(b * size, size)
            scale = alpha[at, :]
            value = attn[at, cols(h)]
            cotangent = g[at, cols(h)].astype(f32)
            normed = value * scale
            out[at, cols(h)] = (normed * gain_h).astype(bf16)
            part = part + jnp.sum(cotangent * normed, axis=0, keepdims=True)
            a = scale * (cotangent * gain_h) - beta[at, :] * value
            attn[at, cols(h)] = a
            high, low = split(a * jnp.exp(cols_g[at, cols(h)]))
            both = dot(q[at, cols(h)], jnp.concatenate([high, low], axis=1), 0, 0)
            mine = both[:, :WIDTH] + both[:, WIDTH:]
            back[h, b] = mine
            state = jnp.exp(total(h, b)) * state + mine
        gparts[z, :, cols(h)] = part
        b_out[h] = state
        store(0, h).start()

        @pl.when(z == seq_count - 1)
        def _():
            b_in[h] = jnp.zeros((WIDTH, WIDTH), f32)
            backward(h).start()
        return carry

    lax.fori_loop(0, heads, gradients, 0)

    def gain_copy(step, slot):
        return pltpu.make_async_remote_copy(
            src_ref=gparts.at[slot], dst_ref=gparts.at[slot], send_sem=g_send.at[step], recv_sem=g_recv.at[step],
            device_id=(lax.rem(z + step, seq_count), me), device_id_type=MESH)

    for step in range(1, seq_count):
        gain_copy(step, z).start()

    def finish(h, carry):
        @pl.when(z < seq_count - 1)
        def _():
            backward(h).wait_recv()

            @pl.when(z > 0)
            def _():
                b_out[h] = b_out[h] + jnp.exp(device_total(h)) * b_in[h]
                backward(h).start()

        state = b_in[h]
        for b in reversed(range(count)):
            at = pl.ds(b * size, size)
            query, key, value = q[at, cols(h)], k[at, cols(h)], v[at, cols(h)]
            a_high, a_low = split(attn[at, cols(h)])
            a_both = jnp.concatenate([a_high, a_low], axis=1)
            ds = dot(a_both, jnp.concatenate([value, value], axis=1), 1, 1) * mask[h, at, :]
            ds_high, ds_low = split(ds)
            column = cols_g[at, cols(h)]
            e_high, e_low = split(entering[h, b])
            cross = dot(a_both, jnp.concatenate([e_high, e_high], axis=1), 1, 1) + dot(a_high, e_low, 1, 1)
            dq[at, cols(h)] = (
                dot(ds_high, key) + dot(ds_low, key) + jnp.exp(column) * cross
            ).astype(bf16)
            to_end = jnp.exp(total(h, b) - column)
            s_high, s_low = split(state)
            from_later = dot(jnp.concatenate([value, value], axis=1), jnp.concatenate([s_high, s_low], axis=1), 1, 1)
            dk[at, cols(h)] = (
                dot(ds_high, query, 0, 0) + dot(ds_low, query, 0, 0) + to_end * from_later
            ).astype(bf16)
            from_later = dot(jnp.concatenate([key, key], axis=1), jnp.concatenate([s_high, s_low], axis=0))
            both = dot(p_high[h, at, :], a_both, 0, 0)
            dv[at, cols(h)] = (
                both[:, :WIDTH] + both[:, WIDTH:] + dot(p_low[h, at, :], a_high, 0, 0) + to_end * from_later
            ).astype(bf16)
            state = jnp.exp(total(h, b)) * state + back[h, b]
        store(1, h).start()
        store(2, h).start()
        store(3, h).start()
        return carry

    lax.fori_loop(0, heads, finish, 0)

    for step in range(1, seq_count):
        gain_copy(step, lax.rem(z + seq_count - step, seq_count)).wait_recv()
    result = gparts[0]
    for d in range(1, seq_count):
        result = result + gparts[d]
    dgain[...] = result

    for step in range(1, seq_count):
        gain_copy(step, z).wait_send()
    for step in range(1, head_count):
        exchange(step).wait_send()
    for h in range(heads):
        for n in range(4):
            store(n, h).wait()

    @pl.when(z < seq_count - 1)
    def _():
        for h in range(heads):
            forward(h).wait_send()

    @pl.when(z > 0)
    def _():
        for h in range(heads):
            backward(h).wait_send()


def local(queries, keys, values, log_decay, gain, out_grad):
    rows, channels = queries.shape
    heads = log_decay.shape[0]
    seq_count, head_count = lax.axis_size("seq"), lax.axis_size("head")
    size = min(256, rows)
    count = rows // size
    any_spec = pl.BlockSpec(memory_space=pl.ANY)
    vmem_spec = pl.BlockSpec(memory_space=pltpu.VMEM)
    narrow = jax.ShapeDtypeStruct((rows, channels), bf16)
    state = pltpu.VMEM((heads, WIDTH, WIDTH), f32)
    block_states = pltpu.VMEM((heads, count, WIDTH, WIDTH), f32)
    dma = pltpu.SemaphoreType.DMA
    results = pl.pallas_call(
        functools.partial(kernel, seq_count, head_count, heads, rows),
        out_shape=(narrow,) * 4 + (jax.ShapeDtypeStruct((1, channels), f32),),
        in_specs=[vmem_spec, vmem_spec] + [any_spec] * 4,
        out_specs=(any_spec,) * 4 + (vmem_spec,),
        scratch_shapes=[pltpu.VMEM((rows, channels), bf16)] * 8
        + [
            pltpu.VMEM((rows, channels), f32),
            pltpu.VMEM((heads, rows), f32),
            pltpu.VMEM((rows, channels), f32),
            block_states, block_states, block_states,
            pltpu.VMEM((heads, rows, size), f32),
            pltpu.VMEM((heads, rows, size), bf16),
            pltpu.VMEM((heads, rows, size), bf16),
            state, state, state, state,
            pltpu.VMEM((rows, WIDTH), f32),
            pltpu.VMEM((rows, WIDTH), f32),
            pltpu.VMEM((head_count, 2, rows), f32),
            pltpu.VMEM((rows, WIDTH), f32),
            pltpu.VMEM((rows, WIDTH), f32),
            pltpu.VMEM((seq_count, 1, channels), f32),
            dma((4, heads)), dma((4, heads)),
            dma((heads,)), dma((heads,)), dma((heads,)), dma((heads,)),
            dma((head_count,)), dma((head_count,)), dma((seq_count,)), dma((seq_count,)),
        ],
        compiler_params=pltpu.CompilerParams(
            collective_id=0, has_side_effects=True, vmem_limit_bytes=60 * 1024 * 1024
        ),
        name="lightning",
    )(log_decay, gain.reshape(1, channels), queries, keys, values, out_grad)
    return results[:4] + (results[4].reshape(channels),)


def solution(mesh):
    in_specs = (
        P("seq", "head"),
        P("seq", "head"),
        P("seq", "head"),
        P("head", "seq"),
        P("head"),
        P("seq", "head"),
    )
    out_specs = (P("seq", "head"), P("seq", "head"), P("seq", "head"), P("seq", "head"), P("head"))
    return jax.shard_map(local, mesh=mesh, in_specs=in_specs, out_specs=out_specs, check_vma=False)
```

time: 290 us -> 72.8 us (0.25); the launches traced: 285 us -> 72.6 us
  matrix products: 84.1 us -> 0 us
  waiting for transfers between devices: 72.5 us -> 0 us
  Pallas kernels: 0 us -> 62.1 us
  local copies, waits for them, and re-layouts: 46.9 us -> 9.84 us
  blocking collectives: 37 us -> 0 us
  other arithmetic: 25.6 us -> 0 us
  starting transfers between devices: 17.4 us -> 0 us
    dot_general x12 -> x0, matrix products: 84.1 us -> none  [the longest x1 20.4 us: local(): jnp.einsum('hnij,hnid->hnjd', scores, attended_grad, precision=highest)]
    ppermute x6 -> x0, waiting for transfers between devices: 72.5 us -> none  [passed_along(): lax.ppermute(value, axis, [(source, source + steps) for source in range(i...]
    pallas_call x0 -> x1, Pallas kernels: none -> 62.1 us  [local(): pl.pallas_call(functools.partial(kernel, seq_count, head_count, heads, ro...]
    psum x3 -> x0, blocking collectives: 37 us -> none  [the longest x1 13.4 us: local(): gain_grad = lax.psum(gain_part, 'seq')]
    ppermute x6 -> x0, starting transfers between devices: 17.4 us -> none  [passed_along(): lax.ppermute(value, axis, [(source, source + steps) for source in range(i...]
    convert_element_type x4 -> x0, local copies, waits for them, and re-layouts: 11.8 us -> none  [the longest x2 6 us: local(): from_blocks(value_grad).astype(jnp.bfloat16)]
    add x8 -> x0, other arithmetic: 9.91 us -> none  [the longest x3 5.85 us: relay_step(): outgoing = jnp.exp(device_decay)[:, None, None] * suffix + device_back]
    transpose x4 -> x0, local copies, waits for them, and re-layouts: 9.04 us -> none  [to_blocks(): matrix.reshape(block_count, block_rows, heads_local, head_width)]
  transfers between devices with their start and end apart: 6 -> 0, of which waited for: 6 -> 0; matrix products, arithmetic and copies ran while one was open for 0% -> 0% of each run, Pallas kernels for 0% -> 0%
where the time goes in v1:
time: 72.8 us; the launch traced here: 72.6 us
  Pallas kernels  62.1 us (85%)
  local copies, waits for them, and re-layouts  9.84 us (14%)
    pallas_call x1, Pallas kernels, local(): pl.pallas_call(functools.partial(kernel, seq_count, head_count, heads, ro...  62.1 us
    unnamed x13, local copies, waits for them, and re-layouts  9.84 us

profile of v1, /device:TPU:0, one launch (start us, length us, event | category | flops | bytes accessed | tf_op | source)
XLA Modules:
  0.0 72.6 jit_solution(13336261310228744175)
XLA Ops:
  0.6 62.1 %lightning.1 = (bf16[1024,1024]{1,0:T(8,128)(2,1)}, bf16[1024,1024]{1,0:T(8,128)(2,1)}, bf16[1024,1024]{1,0:T(8,128)(2,1)}, bf16[1024,1024]{1,0:T(8,128)(2,1)}, f32[1,1024]{1,0:T(1,128)}) custom-call(f32[8,1024]{1,0:T(8,128)} %decay.1, f32[1,1024]{1,0:T(1,128)} %bitcast.2, bf16[1024,1024]{1,0:T(8,128)(2,1)} %q_hbm.1, bf16[1024,1024]{1,0:T(8,128)(2,1)} %k_hbm.1, ...), custom_call_target="tpu_custom_call" | custom-call | tf_op jit(solution)/shard_map/lightning/pallas_call | solution.py:306
  62.7 0.0 copy-start.2
  62.7 3.2 %copy.16 = bf16[1024,1024]{1,0:T(8,128)(2,1)} copy(bf16[1024,1024]{1,0:T(8,128)(2,1)} %get-tuple-element.20) | data formatting | bytes 4194304
  66.0 0.0 copy-done.2
  66.0 0.0 copy-start.1
  66.0 1.3 %copy.17 = bf16[1024,1024]{1,0:T(8,128)(2,1)} copy(bf16[1024,1024]{1,0:T(8,128)(2,1)S(1)} %copy-done.2) | data formatting | bytes 4194304
  67.3 1.0 %copy-done.1 = bf16[1024,1024]{1,0:T(8,128)(2,1)S(1)} copy-done((bf16[1024,1024]{1,0:T(8,128)(2,1)S(1)}, bf16[1024,1024]{1,0:T(8,128)(2,1)}, u32[]{:S(2)}) %copy-start.1) | copy-done | bytes 2097176
  68.3 0.0 copy-start
  68.3 1.3 %copy.18 = bf16[1024,1024]{1,0:T(8,128)(2,1)} copy(bf16[1024,1024]{1,0:T(8,128)(2,1)S(1)} %copy-done.1) | data formatting | bytes 4194304
  69.6 1.0 %copy-done = bf16[1024,1024]{1,0:T(8,128)(2,1)S(1)} copy-done((bf16[1024,1024]{1,0:T(8,128)(2,1)S(1)}, bf16[1024,1024]{1,0:T(8,128)(2,1)}, u32[]{:S(2)}) %copy-start) | copy-done | bytes 2097176
  70.7 0.0 copy-start.3
  70.7 1.3 %copy.19 = bf16[1024,1024]{1,0:T(8,128)(2,1)} copy(bf16[1024,1024]{1,0:T(8,128)(2,1)S(1)} %copy-done) | data formatting | bytes 4194304
  72.0 0.0 copy-done.3
  72.0 0.6 copy.20
Async XLA Ops:
  62.7 3.2 %copy-start.2 = (bf16[1024,1024]{1,0:T(8,128)(2,1)S(1)}, bf16[1024,1024]{1,0:T(8,128)(2,1)}, u32[]{:S(2)}) copy-start(bf16[1024,1024]{1,0:T(8,128)(2,1)} %get-tuple-element.21) | copy-start | bytes 6291460
  66.0 2.3 %copy-start.1 = (bf16[1024,1024]{1,0:T(8,128)(2,1)S(1)}, bf16[1024,1024]{1,0:T(8,128)(2,1)}, u32[]{:S(2)}) copy-start(bf16[1024,1024]{1,0:T(8,128)(2,1)} %get-tuple-element.22) | copy-start | bytes 6291460
  68.3 2.3 %copy-start = (bf16[1024,1024]{1,0:T(8,128)(2,1)S(1)}, bf16[1024,1024]{1,0:T(8,128)(2,1)}, u32[]{:S(2)}) copy-start(bf16[1024,1024]{1,0:T(8,128)(2,1)} %get-tuple-element.23) | copy-start | bytes 6291460
  70.7 1.3 %copy-start.3 = (f32[1,1024]{1,0:T(1,128)S(1)}, f32[1,1024]{1,0:T(1,128)}, u32[]{:S(2)}) copy-start(f32[1,1024]{1,0:T(1,128)} %get-tuple-element.14) | copy-start | bytes 12292

commit v2 on v1

--- a/solution.py
+++ b/solution.py
@@ -115,7 +115,7 @@
             result = result + total(h, b)
         return result
 
-    def attend(h, carry):
+    def attend(h):
         load(2, h).wait()
         load(3, h).wait()
         for b in range(count):
@@ -124,10 +124,11 @@
             m = jnp.exp(jnp.where(below, wide - sums_g[pl.ds(h, 1), at], -1e30))
             mask[h, at, :] = m
             high, low = split(dot(q[at, cols(h)], k[at, cols(h)], 1, 1) * m)
-            p_high[h, at, :] = high
-            p_low[h, at, :] = low
+            p_high[h, at, :] = high.T
+            p_low[h, at, :] = low.T
             attn[at, cols(h)] = dot(high, v[at, cols(h)]) + dot(low, v[at, cols(h)])
 
+    def enter(h):
         @pl.when(z > 0)
         def _():
             forward(h).wait_recv()
@@ -149,9 +150,20 @@
             acc_sq[at, :] = acc_sq[at, :] + value * value
             acc_pr[at, :] = acc_pr[at, :] + value * (g[at, cols(h)].astype(f32) * gain[:, cols(h)])
             state = jnp.exp(total(h, b)) * state + own[h, b]
+
+    lag = jnp.where(z == 0, 0, jnp.minimum(heads, 3 * z - 1))
+
+    def forward_step(i, carry):
+        @pl.when(i < heads)
+        def _():
+            attend(i)
+
+        @pl.when(i >= lag)
+        def _():
+            enter(i - lag)
         return carry
 
-    lax.fori_loop(0, heads, attend, 0)
+    lax.fori_loop(0, heads + lag, forward_step, 0)
 
     for b in range(rows // WIDTH):
         at = pl.ds(b * WIDTH, WIDTH)
@@ -222,18 +234,13 @@
     for step in range(1, seq_count):
         gain_copy(step, z).start()
 
-    def finish(h, carry):
-        @pl.when(z < seq_count - 1)
-        def _():
-            backward(h).wait_recv()
-
-            @pl.when(z > 0)
-            def _():
-                b_out[h] = b_out[h] + jnp.exp(device_total(h)) * b_in[h]
-                backward(h).start()
-
-        state = b_in[h]
-        for b in reversed(range(count)):
+    def relay(h):
+        backward(h).wait_recv()
+        b_out[h] = b_out[h] + jnp.exp(device_total(h)) * b_in[h]
+        backward(h).start()
+
+    def inside_gradients(h):
+        for b in range(count):
             at = pl.ds(b * size, size)
             query, key, value = q[at, cols(h)], k[at, cols(h)], v[at, cols(h)]
             a_high, a_low = split(attn[at, cols(h)])
@@ -246,24 +253,51 @@
             dq[at, cols(h)] = (
                 dot(ds_high, key) + dot(ds_low, key) + jnp.exp(column) * cross
             ).astype(bf16)
-            to_end = jnp.exp(total(h, b) - column)
+            mask[h, at, 0:WIDTH] = dot(ds_high, query, 0, 0) + dot(ds_low, query, 0, 0)
+            both = dot(p_high[h, at, :], a_both)
+            mask[h, at, WIDTH:2 * WIDTH] = both[:, :WIDTH] + both[:, WIDTH:] + dot(p_low[h, at, :], a_high)
+        store(1, h).start()
+
+    def leave(h):
+        @pl.when(z == 0)
+        def _():
+            backward(h).wait_recv()
+
+        state = b_in[h]
+        for b in reversed(range(count)):
+            at = pl.ds(b * size, size)
+            key, value = k[at, cols(h)], v[at, cols(h)]
+            to_end = jnp.exp(total(h, b) - cols_g[at, cols(h)])
             s_high, s_low = split(state)
             from_later = dot(jnp.concatenate([value, value], axis=1), jnp.concatenate([s_high, s_low], axis=1), 1, 1)
-            dk[at, cols(h)] = (
-                dot(ds_high, query, 0, 0) + dot(ds_low, query, 0, 0) + to_end * from_later
-            ).astype(bf16)
+            dk[at, cols(h)] = (mask[h, at, 0:WIDTH] + to_end * from_later).astype(bf16)
             from_later = dot(jnp.concatenate([key, key], axis=1), jnp.concatenate([s_high, s_low], axis=0))
-            both = dot(p_high[h, at, :], a_both, 0, 0)
-            dv[at, cols(h)] = (
-                both[:, :WIDTH] + both[:, WIDTH:] + dot(p_low[h, at, :], a_high, 0, 0) + to_end * from_later
-            ).astype(bf16)
+            dv[at, cols(h)] = (mask[h, at, WIDTH:2 * WIDTH] + to_end * from_later).astype(bf16)
             state = jnp.exp(total(h, b)) * state + back[h, b]
-        store(1, h).start()
         store(2, h).start()
         store(3, h).start()
+
+    late = jnp.where(z == seq_count - 1, 0, jnp.minimum(heads, 1 + 2 * (seq_count - 2 - z)))
+    between = jnp.logical_and(z > 0, z < seq_count - 1)
+
+    def backward_step(i, carry):
+        for r in range(2):
+            j = 2 * (i - late) + r
+
+            @pl.when(jnp.logical_and(between, jnp.logical_and(j >= 0, j < heads)))
+            def _():
+                relay(j)
+
+        @pl.when(i < heads)
+        def _():
+            inside_gradients(i)
+
+        @pl.when(i >= late)
+        def _():
+            leave(i - late)
         return carry
 
-    lax.fori_loop(0, heads, finish, 0)
+    lax.fori_loop(0, heads + late, backward_step, 0)
 
     for step in range(1, seq_count):
         gain_copy(step, lax.rem(z + seq_count - step, seq_count)).wait_recv()

time: 72.8 us -> 69.3 us (0.952)
  Pallas kernels: 62.1 us -> 58.6 us
    pallas_call x1, Pallas kernels: 62.1 us -> 58.6 us  [local(): pl.pallas_call(functools.partial(kernel, seq_count, head_count, heads, ro...]
where the time goes in v2:
time: 69.3 us; the launch traced here: 69.1 us
  Pallas kernels  58.6 us (85%)
  local copies, waits for them, and re-layouts  9.84 us (14%)
    pallas_call x1, Pallas kernels, local(): pl.pallas_call(functools.partial(kernel, seq_count, head_count, heads, ro...  58.6 us
    unnamed x13, local copies, waits for them, and re-layouts  9.84 us

profile of v2, /device:TPU:0, one launch (start us, length us, event | category | flops | bytes accessed | tf_op | source)
XLA Modules:
  0.0 69.1 jit_solution(5663339265329279386)
XLA Ops:
  0.6 58.6 %lightning.1 = (bf16[1024,1024]{1,0:T(8,128)(2,1)}, bf16[1024,1024]{1,0:T(8,128)(2,1)}, bf16[1024,1024]{1,0:T(8,128)(2,1)}, bf16[1024,1024]{1,0:T(8,128)(2,1)}, f32[1,1024]{1,0:T(1,128)}) custom-call(f32[8,1024]{1,0:T(8,128)} %decay.1, f32[1,1024]{1,0:T(1,128)} %bitcast.2, bf16[1024,1024]{1,0:T(8,128)(2,1)} %q_hbm.1, bf16[1024,1024]{1,0:T(8,128)(2,1)} %k_hbm.1, ...), custom_call_target="tpu_custom_call" | custom-call | tf_op jit(solution)/shard_map/lightning/pallas_call | solution.py:340
  59.2 0.0 copy-start.2
  59.2 3.2 %copy.16 = bf16[1024,1024]{1,0:T(8,128)(2,1)} copy(bf16[1024,1024]{1,0:T(8,128)(2,1)} %get-tuple-element.20) | data formatting | bytes 4194304
  62.4 0.0 copy-done.2
  62.5 0.0 copy-start.1
  62.5 1.3 %copy.17 = bf16[1024,1024]{1,0:T(8,128)(2,1)} copy(bf16[1024,1024]{1,0:T(8,128)(2,1)S(1)} %copy-done.2) | data formatting | bytes 4194304
  63.8 1.0 %copy-done.1 = bf16[1024,1024]{1,0:T(8,128)(2,1)S(1)} copy-done((bf16[1024,1024]{1,0:T(8,128)(2,1)S(1)}, bf16[1024,1024]{1,0:T(8,128)(2,1)}, u32[]{:S(2)}) %copy-start.1) | copy-done | bytes 2097176
  64.8 0.0 copy-start
  64.8 1.3 %copy.18 = bf16[1024,1024]{1,0:T(8,128)(2,1)} copy(bf16[1024,1024]{1,0:T(8,128)(2,1)S(1)} %copy-done.1) | data formatting | bytes 4194304
  66.1 1.0 %copy-done = bf16[1024,1024]{1,0:T(8,128)(2,1)S(1)} copy-done((bf16[1024,1024]{1,0:T(8,128)(2,1)S(1)}, bf16[1024,1024]{1,0:T(8,128)(2,1)}, u32[]{:S(2)}) %copy-start) | copy-done | bytes 2097176
  67.1 0.0 copy-start.3
  67.2 1.3 %copy.19 = bf16[1024,1024]{1,0:T(8,128)(2,1)} copy(bf16[1024,1024]{1,0:T(8,128)(2,1)S(1)} %copy-done) | data formatting | bytes 4194304
  68.5 0.0 copy-done.3
  68.5 0.6 copy.20
Async XLA Ops:
  59.2 3.2 %copy-start.2 = (bf16[1024,1024]{1,0:T(8,128)(2,1)S(1)}, bf16[1024,1024]{1,0:T(8,128)(2,1)}, u32[]{:S(2)}) copy-start(bf16[1024,1024]{1,0:T(8,128)(2,1)} %get-tuple-element.21) | copy-start | bytes 6291460
  62.5 2.3 %copy-start.1 = (bf16[1024,1024]{1,0:T(8,128)(2,1)S(1)}, bf16[1024,1024]{1,0:T(8,128)(2,1)}, u32[]{:S(2)}) copy-start(bf16[1024,1024]{1,0:T(8,128)(2,1)} %get-tuple-element.22) | copy-start | bytes 6291460
  64.8 2.3 %copy-start = (bf16[1024,1024]{1,0:T(8,128)(2,1)S(1)}, bf16[1024,1024]{1,0:T(8,128)(2,1)}, u32[]{:S(2)}) copy-start(bf16[1024,1024]{1,0:T(8,128)(2,1)} %get-tuple-element.23) | copy-start | bytes 6291460
  67.1 1.3 %copy-start.3 = (f32[1,1024]{1,0:T(1,128)S(1)}, f32[1,1024]{1,0:T(1,128)}, u32[]{:S(2)}) copy-start(f32[1,1024]{1,0:T(1,128)} %get-tuple-element.14) | copy-start | bytes 12292

commit v3 on v2

--- a/solution.py
+++ b/solution.py
@@ -28,13 +28,13 @@
     decay, gain, q_hbm, k_hbm, v_hbm, g_hbm,
     out_hbm, dq_hbm, dk_hbm, dv_hbm, dgain,
     q, k, v, g, out, dq, dk, dv,
-    attn, sums_g, cols_g, own, entering, back, mask, p_high, p_low,
+    attn, sums_g, cols_g, ends, own, entering, back, mask, p_high, p_low,
     f_in, f_out, b_in, b_out, acc_sq, acc_pr, norm, alpha, beta, gparts,
     in_sem, out_sem, f_send, f_recv, b_send, b_recv, n_send, n_recv, g_send, g_recv,
 ):
     z = lax.axis_index("seq")
     me = lax.axis_index("head")
-    size = min(256, rows)
+    size = min(128, rows)
     count = rows // size
     channels = heads * WIDTH * head_count
 
@@ -77,12 +77,14 @@
     tri = jnp.where(above, 1.0, 0.0).astype(f32)
     for b in range(count):
         at = pl.ds(b * size, size)
-        sums_g[:, at] = jnp.dot(decay[:, at], tri, precision=highest, preferred_element_type=f32)
+        along = jnp.dot(decay[:, at], tri, precision=highest, preferred_element_type=f32)
+        for h in range(heads):
+            sums_g[h, :, at] = along[h:h + 1]
     acc_sq[...] = jnp.zeros_like(acc_sq)
     acc_pr[...] = jnp.zeros_like(acc_pr)
     pl.semaphore_wait(barrier, head_count - 1 + seq_count - 1)
 
-    def total(h, b):
+    def factor(h, b):
         return cols_g[(b + 1) * size - 1:(b + 1) * size, cols(h)]
 
     def states(h, carry):
@@ -91,10 +93,12 @@
         state = jnp.zeros((WIDTH, WIDTH), f32)
         for b in range(count):
             at = pl.ds(b * size, size)
-            column = jnp.broadcast_to(sums_g[pl.ds(h, 1), at], (WIDTH, size)).T
+            column = jnp.broadcast_to(sums_g[h, :, at], (WIDTH, size)).T
             cols_g[at, cols(h)] = column
             last = column[size - 1:size, :]
-            high, low = split(v[at, cols(h)].astype(f32) * jnp.exp(last - column))
+            to_end = jnp.exp(last - column)
+            ends[at, cols(h)] = to_end
+            high, low = split(v[at, cols(h)].astype(f32) * to_end)
             both = dot(k[at, cols(h)], jnp.concatenate([high, low], axis=1), 0, 0)
             mine = both[:, :WIDTH] + both[:, WIDTH:]
             own[h, b] = mine
@@ -109,10 +113,10 @@
 
     lax.fori_loop(0, heads, states, 0)
 
-    def device_total(h):
-        result = total(h, 0)
+    def device_factor(h):
+        result = factor(h, 0)
         for b in range(1, count):
-            result = result + total(h, b)
+            result = result * factor(h, b)
         return result
 
     def attend(h):
@@ -120,13 +124,17 @@
         load(3, h).wait()
         for b in range(count):
             at = pl.ds(b * size, size)
-            wide = jnp.concatenate([cols_g[at, cols(h)]] * (size // WIDTH), axis=1)
-            m = jnp.exp(jnp.where(below, wide - sums_g[pl.ds(h, 1), at], -1e30))
+            column = cols_g[at, cols(h)]
+            m = jnp.exp(jnp.where(below, column - sums_g[h, :, at], -1e30))
+            cols_g[at, cols(h)] = jnp.exp(column)
             mask[h, at, :] = m
             high, low = split(dot(q[at, cols(h)], k[at, cols(h)], 1, 1) * m)
             p_high[h, at, :] = high.T
             p_low[h, at, :] = low.T
-            attn[at, cols(h)] = dot(high, v[at, cols(h)]) + dot(low, v[at, cols(h)])
+            value = v[at, cols(h)]
+            attn[at, cols(h)] = dot(
+                jnp.concatenate([high, low], axis=1), jnp.concatenate([value, value], axis=0)
+            )
 
     def enter(h):
         @pl.when(z > 0)
@@ -135,7 +143,7 @@
 
             @pl.when(z < seq_count - 1)
             def _():
-                f_out[h] = f_out[h] + jnp.exp(device_total(h)) * f_in[h]
+                f_out[h] = f_out[h] + device_factor(h) * f_in[h]
                 forward(h).start()
 
         state = f_in[h]
@@ -145,11 +153,11 @@
             high, low = split(state)
             query = q[at, cols(h)]
             cross = dot(jnp.concatenate([query, query], axis=1), jnp.concatenate([high, low], axis=0))
-            value = attn[at, cols(h)] + jnp.exp(cols_g[at, cols(h)]) * cross
+            value = attn[at, cols(h)] + cols_g[at, cols(h)] * cross
             attn[at, cols(h)] = value
             acc_sq[at, :] = acc_sq[at, :] + value * value
             acc_pr[at, :] = acc_pr[at, :] + value * (g[at, cols(h)].astype(f32) * gain[:, cols(h)])
-            state = jnp.exp(total(h, b)) * state + own[h, b]
+            state = factor(h, b) * state + own[h, b]
 
     lag = jnp.where(z == 0, 0, jnp.minimum(heads, 3 * z - 1))
 
@@ -209,11 +217,11 @@
             part = part + jnp.sum(cotangent * normed, axis=0, keepdims=True)
             a = scale * (cotangent * gain_h) - beta[at, :] * value
             attn[at, cols(h)] = a
-            high, low = split(a * jnp.exp(cols_g[at, cols(h)]))
+            high, low = split(a * cols_g[at, cols(h)])
             both = dot(q[at, cols(h)], jnp.concatenate([high, low], axis=1), 0, 0)
             mine = both[:, :WIDTH] + both[:, WIDTH:]
             back[h, b] = mine
-            state = jnp.exp(total(h, b)) * state + mine
+            state = factor(h, b) * state + mine
         gparts[z, :, cols(h)] = part
         b_out[h] = state
         store(0, h).start()
@@ -236,7 +244,7 @@
 
     def relay(h):
         backward(h).wait_recv()
-        b_out[h] = b_out[h] + jnp.exp(device_total(h)) * b_in[h]
+        b_out[h] = b_out[h] + device_factor(h) * b_in[h]
         backward(h).start()
 
     def inside_gradients(h):
@@ -245,17 +253,25 @@
             query, key, value = q[at, cols(h)], k[at, cols(h)], v[at, cols(h)]
             a_high, a_low = split(attn[at, cols(h)])
             a_both = jnp.concatenate([a_high, a_low], axis=1)
-            ds = dot(a_both, jnp.concatenate([value, value], axis=1), 1, 1) * mask[h, at, :]
-            ds_high, ds_low = split(ds)
-            column = cols_g[at, cols(h)]
             e_high, e_low = split(entering[h, b])
-            cross = dot(a_both, jnp.concatenate([e_high, e_high], axis=1), 1, 1) + dot(a_high, e_low, 1, 1)
+            right = jnp.concatenate(
+                [jnp.concatenate([value, value], axis=1), jnp.concatenate([e_high, e_high], axis=1)], axis=0
+            )
+            both = dot(a_both, right, 1, 1)
+            ds_high, ds_low = split(both[:, :size] * mask[h, at, :])
+            cross = both[:, size:] + dot(a_high, e_low, 1, 1)
             dq[at, cols(h)] = (
-                dot(ds_high, key) + dot(ds_low, key) + jnp.exp(column) * cross
+                dot(jnp.concatenate([ds_high, ds_low], axis=1), jnp.concatenate([key, key], axis=0))
+                + cols_g[at, cols(h)] * cross
             ).astype(bf16)
-            mask[h, at, 0:WIDTH] = dot(ds_high, query, 0, 0) + dot(ds_low, query, 0, 0)
-            both = dot(p_high[h, at, :], a_both)
-            mask[h, at, WIDTH:2 * WIDTH] = both[:, :WIDTH] + both[:, WIDTH:] + dot(p_low[h, at, :], a_high)
+            mask[h, at, :] = dot(
+                jnp.concatenate([ds_high, ds_low], axis=0), jnp.concatenate([query, query], axis=0), 0, 0
+            )
+            right = jnp.concatenate(
+                [a_both, jnp.concatenate([a_high, jnp.zeros_like(a_high)], axis=1)], axis=0
+            )
+            both = dot(jnp.concatenate([p_high[h, at, :], p_low[h, at, :]], axis=1), right)
+            attn[at, cols(h)] = both[:, :WIDTH] + both[:, WIDTH:]
         store(1, h).start()
 
     def leave(h):
@@ -267,13 +283,13 @@
         for b in reversed(range(count)):
             at = pl.ds(b * size, size)
             key, value = k[at, cols(h)], v[at, cols(h)]
-            to_end = jnp.exp(total(h, b) - cols_g[at, cols(h)])
+            to_end = ends[at, cols(h)]
             s_high, s_low = split(state)
             from_later = dot(jnp.concatenate([value, value], axis=1), jnp.concatenate([s_high, s_low], axis=1), 1, 1)
-            dk[at, cols(h)] = (mask[h, at, 0:WIDTH] + to_end * from_later).astype(bf16)
+            dk[at, cols(h)] = (mask[h, at, :] + to_end * from_later).astype(bf16)
             from_later = dot(jnp.concatenate([key, key], axis=1), jnp.concatenate([s_high, s_low], axis=0))
-            dv[at, cols(h)] = (mask[h, at, WIDTH:2 * WIDTH] + to_end * from_later).astype(bf16)
-            state = jnp.exp(total(h, b)) * state + back[h, b]
+            dv[at, cols(h)] = (attn[at, cols(h)] + to_end * from_later).astype(bf16)
+            state = factor(h, b) * state + back[h, b]
         store(2, h).start()
         store(3, h).start()
 
@@ -329,7 +345,7 @@
     rows, channels = queries.shape
     heads = log_decay.shape[0]
     seq_count, head_count = lax.axis_size("seq"), lax.axis_size("head")
-    size = min(256, rows)
+    size = min(128, rows)
     count = rows // size
     any_spec = pl.BlockSpec(memory_space=pl.ANY)
     vmem_spec = pl.BlockSpec(memory_space=pltpu.VMEM)
@@ -345,7 +361,8 @@
         scratch_shapes=[pltpu.VMEM((rows, channels), bf16)] * 8
         + [
             pltpu.VMEM((rows, channels), f32),
-            pltpu.VMEM((heads, rows), f32),
+            pltpu.VMEM((heads, 1, rows), f32),
+            pltpu.VMEM((rows, channels), f32),
             pltpu.VMEM((rows, channels), f32),
             block_states, block_states, block_states,
             pltpu.VMEM((heads, rows, size), f32),

time: 69.3 us -> 75.5 us (1.089); the launches traced: 69.1 us -> 74 us
  Pallas kernels: 58.6 us -> 63.5 us
    pallas_call x1, Pallas kernels: 58.6 us -> 63.5 us  [local(): pl.pallas_call(functools.partial(kernel, seq_count, head_count, heads, ro...]
where the time goes in v3:
time: 75.5 us; the launch traced here: 74 us
  Pallas kernels  63.5 us (84%)
  local copies, waits for them, and re-layouts  9.84 us (13%)
    pallas_call x1, Pallas kernels, local(): pl.pallas_call(functools.partial(kernel, seq_count, head_count, heads, ro...  63.5 us
    unnamed x13, local copies, waits for them, and re-layouts  9.84 us

profile of v3, /device:TPU:0, one launch (start us, length us, event | category | flops | bytes accessed | tf_op | source)
XLA Modules:
  0.0 74.0 jit_solution(14934816353573426694)
XLA Ops:
  0.6 63.5 %lightning.1 = (bf16[1024,1024]{1,0:T(8,128)(2,1)}, bf16[1024,1024]{1,0:T(8,128)(2,1)}, bf16[1024,1024]{1,0:T(8,128)(2,1)}, bf16[1024,1024]{1,0:T(8,128)(2,1)}, f32[1,1024]{1,0:T(1,128)}) custom-call(f32[8,1024]{1,0:T(8,128)} %decay.1, f32[1,1024]{1,0:T(1,128)} %bitcast.2, bf16[1024,1024]{1,0:T(8,128)(2,1)} %q_hbm.1, bf16[1024,1024]{1,0:T(8,128)(2,1)} %k_hbm.1, ...), custom_call_target="tpu_custom_call" | custom-call | tf_op jit(solution)/shard_map/lightning/pallas_call | solution.py:356
  64.1 0.0 copy-start.2
  64.1 3.2 %copy.16 = bf16[1024,1024]{1,0:T(8,128)(2,1)} copy(bf16[1024,1024]{1,0:T(8,128)(2,1)} %get-tuple-element.20) | data formatting | bytes 4194304
  67.4 0.0 copy-done.2
  67.4 0.0 copy-start.1
  67.4 1.3 %copy.17 = bf16[1024,1024]{1,0:T(8,128)(2,1)} copy(bf16[1024,1024]{1,0:T(8,128)(2,1)S(1)} %copy-done.2) | data formatting | bytes 4194304
  68.7 1.0 %copy-done.1 = bf16[1024,1024]{1,0:T(8,128)(2,1)S(1)} copy-done((bf16[1024,1024]{1,0:T(8,128)(2,1)S(1)}, bf16[1024,1024]{1,0:T(8,128)(2,1)}, u32[]{:S(2)}) %copy-start.1) | copy-done | bytes 2097176
  69.7 0.0 copy-start
  69.7 1.3 %copy.18 = bf16[1024,1024]{1,0:T(8,128)(2,1)} copy(bf16[1024,1024]{1,0:T(8,128)(2,1)S(1)} %copy-done.1) | data formatting | bytes 4194304
  71.0 1.0 %copy-done = bf16[1024,1024]{1,0:T(8,128)(2,1)S(1)} copy-done((bf16[1024,1024]{1,0:T(8,128)(2,1)S(1)}, bf16[1024,1024]{1,0:T(8,128)(2,1)}, u32[]{:S(2)}) %copy-start) | copy-done | bytes 2097176
  72.1 0.0 copy-start.3
  72.1 1.3 %copy.19 = bf16[1024,1024]{1,0:T(8,128)(2,1)} copy(bf16[1024,1024]{1,0:T(8,128)(2,1)S(1)} %copy-done) | data formatting | bytes 4194304
  73.4 0.0 copy-done.3
  73.4 0.6 copy.20
Async XLA Ops:
  64.1 3.2 %copy-start.2 = (bf16[1024,1024]{1,0:T(8,128)(2,1)S(1)}, bf16[1024,1024]{1,0:T(8,128)(2,1)}, u32[]{:S(2)}) copy-start(bf16[1024,1024]{1,0:T(8,128)(2,1)} %get-tuple-element.21) | copy-start | bytes 6291460
  67.4 2.3 %copy-start.1 = (bf16[1024,1024]{1,0:T(8,128)(2,1)S(1)}, bf16[1024,1024]{1,0:T(8,128)(2,1)}, u32[]{:S(2)}) copy-start(bf16[1024,1024]{1,0:T(8,128)(2,1)} %get-tuple-element.22) | copy-start | bytes 6291460
  69.7 2.3 %copy-start = (bf16[1024,1024]{1,0:T(8,128)(2,1)S(1)}, bf16[1024,1024]{1,0:T(8,128)(2,1)}, u32[]{:S(2)}) copy-start(bf16[1024,1024]{1,0:T(8,128)(2,1)} %get-tuple-element.23) | copy-start | bytes 6291460
  72.1 1.3 %copy-start.3 = (f32[1,1024]{1,0:T(1,128)S(1)}, f32[1,1024]{1,0:T(1,128)}, u32[]{:S(2)}) copy-start(f32[1,1024]{1,0:T(1,128)} %get-tuple-element.14) | copy-start | bytes 12292

commit v4 on v3

--- a/solution.py
+++ b/solution.py
@@ -34,9 +34,15 @@
 ):
     z = lax.axis_index("seq")
     me = lax.axis_index("head")
-    size = min(128, rows)
+    size = min(256, rows)
     count = rows // size
     channels = heads * WIDTH * head_count
+
+    spans = [pl.ds(b * size, size) for b in range(count)]
+    blocks = range(count)
+
+    def halves(x):
+        return x[:, :WIDTH] + x[:, WIDTH:]
 
     def cols(h):
         return pl.ds(pl.multiple_of(h * WIDTH, WIDTH), WIDTH)
@@ -90,19 +96,20 @@
     def states(h, carry):
         load(0, h).wait()
         load(1, h).wait()
+        values = [v[at, cols(h)].astype(f32) for at in spans]
+        key_blocks = [k[at, cols(h)] for at in spans]
+        columns = [jnp.broadcast_to(sums_g[h, :, at], (WIDTH, size)).T for at in spans]
+        lasts = [column[size - 1:size, :] for column in columns]
+        to_ends = [jnp.exp(lasts[b] - columns[b]) for b in blocks]
+        sides = [jnp.concatenate(split(values[b] * to_ends[b]), axis=1) for b in blocks]
+        mine = [halves(dot(key_blocks[b], sides[b], 0, 0)) for b in blocks]
         state = jnp.zeros((WIDTH, WIDTH), f32)
-        for b in range(count):
-            at = pl.ds(b * size, size)
-            column = jnp.broadcast_to(sums_g[h, :, at], (WIDTH, size)).T
-            cols_g[at, cols(h)] = column
-            last = column[size - 1:size, :]
-            to_end = jnp.exp(last - column)
-            ends[at, cols(h)] = to_end
-            high, low = split(v[at, cols(h)].astype(f32) * to_end)
-            both = dot(k[at, cols(h)], jnp.concatenate([high, low], axis=1), 0, 0)
-            mine = both[:, :WIDTH] + both[:, WIDTH:]
-            own[h, b] = mine
-            state = jnp.exp(last) * state + mine
+        for b in blocks:
+            state = jnp.exp(lasts[b]) * state + mine[b]
+        for b in blocks:
+            cols_g[spans[b], cols(h)] = columns[b]
+            ends[spans[b], cols(h)] = to_ends[b]
+            own[h, b] = mine[b]
         f_out[h] = state
 
         @pl.when(z == 0)
@@ -122,19 +129,25 @@
     def attend(h):
         load(2, h).wait()
         load(3, h).wait()
-        for b in range(count):
-            at = pl.ds(b * size, size)
-            column = cols_g[at, cols(h)]
-            m = jnp.exp(jnp.where(below, column - sums_g[h, :, at], -1e30))
-            cols_g[at, cols(h)] = jnp.exp(column)
-            mask[h, at, :] = m
-            high, low = split(dot(q[at, cols(h)], k[at, cols(h)], 1, 1) * m)
-            p_high[h, at, :] = high.T
-            p_low[h, at, :] = low.T
-            value = v[at, cols(h)]
-            attn[at, cols(h)] = dot(
-                jnp.concatenate([high, low], axis=1), jnp.concatenate([value, value], axis=0)
-            )
+        columns = [cols_g[at, cols(h)] for at in spans]
+        across = [sums_g[h, :, at] for at in spans]
+        query_blocks = [q[at, cols(h)] for at in spans]
+        key_blocks = [k[at, cols(h)] for at in spans]
+        value_blocks = [v[at, cols(h)] for at in spans]
+        scores = [dot(query_blocks[b], key_blocks[b], 1, 1) for b in blocks]
+        masks = [
+            jnp.exp(jnp.where(below, jnp.concatenate([columns[b]] * (size // WIDTH), axis=1) - across[b], -1e30))
+            for b in blocks
+        ]
+        parts = [split(scores[b] * masks[b]) for b in blocks]
+        inside = [dot(parts[b][0], value_blocks[b]) + dot(parts[b][1], value_blocks[b]) for b in blocks]
+        for b in blocks:
+            at = spans[b]
+            mask[h, at, :] = masks[b]
+            p_high[h, at, :] = parts[b][0].T
+            p_low[h, at, :] = parts[b][1].T
+            attn[at, cols(h)] = inside[b]
+            cols_g[at, cols(h)] = jnp.exp(columns[b])
 
     def enter(h):
         @pl.when(z > 0)
@@ -147,17 +160,27 @@
                 forward(h).start()
 
         state = f_in[h]
-        for b in range(count):
-            at = pl.ds(b * size, size)
-            entering[h, b] = state
-            high, low = split(state)
-            query = q[at, cols(h)]
-            cross = dot(jnp.concatenate([query, query], axis=1), jnp.concatenate([high, low], axis=0))
-            value = attn[at, cols(h)] + cols_g[at, cols(h)] * cross
-            attn[at, cols(h)] = value
-            acc_sq[at, :] = acc_sq[at, :] + value * value
-            acc_pr[at, :] = acc_pr[at, :] + value * (g[at, cols(h)].astype(f32) * gain[:, cols(h)])
-            state = factor(h, b) * state + own[h, b]
+        factors = [factor(h, b) for b in blocks]
+        own_blocks = [own[h, b] for b in blocks]
+        query_blocks = [q[at, cols(h)] for at in spans]
+        inside = [attn[at, cols(h)] for at in spans]
+        starts = [cols_g[at, cols(h)] for at in spans]
+        weights = [g[at, cols(h)].astype(f32) * gain[:, cols(h)] for at in spans]
+        before = []
+        for b in blocks:
+            before.append(state)
+            state = factors[b] * state + own_blocks[b]
+        crosses = [
+            dot(jnp.concatenate([query_blocks[b]] * 2, axis=1), jnp.concatenate(split(before[b]), axis=0))
+            for b in blocks
+        ]
+        results = [inside[b] + starts[b] * crosses[b] for b in blocks]
+        for b in blocks:
+            at = spans[b]
+            entering[h, b] = before[b]
+            attn[at, cols(h)] = results[b]
+            acc_sq[at, :] = acc_sq[at, :] + results[b] * results[b]
+            acc_pr[at, :] = acc_pr[at, :] + results[b] * weights[b]
 
     lag = jnp.where(z == 0, 0, jnp.minimum(heads, 3 * z - 1))
 
@@ -207,21 +230,27 @@
         gain_h = gain[:, cols(h)]
         part = jnp.zeros((1, WIDTH), f32)
         state = jnp.zeros((WIDTH, WIDTH), f32)
-        for b in reversed(range(count)):
-            at = pl.ds(b * size, size)
-            scale = alpha[at, :]
-            value = attn[at, cols(h)]
-            cotangent = g[at, cols(h)].astype(f32)
-            normed = value * scale
-            out[at, cols(h)] = (normed * gain_h).astype(bf16)
-            part = part + jnp.sum(cotangent * normed, axis=0, keepdims=True)
-            a = scale * (cotangent * gain_h) - beta[at, :] * value
-            attn[at, cols(h)] = a
-            high, low = split(a * cols_g[at, cols(h)])
-            both = dot(q[at, cols(h)], jnp.concatenate([high, low], axis=1), 0, 0)
-            mine = both[:, :WIDTH] + both[:, WIDTH:]
-            back[h, b] = mine
-            state = factor(h, b) * state + mine
+        factors = [factor(h, b) for b in blocks]
+        scales = [alpha[at, :] for at in spans]
+        seconds = [beta[at, :] for at in spans]
+        attended = [attn[at, cols(h)] for at in spans]
+        cotangents = [g[at, cols(h)].astype(f32) for at in spans]
+        starts = [cols_g[at, cols(h)] for at in spans]
+        query_blocks = [q[at, cols(h)] for at in spans]
+        grads = [
+            scales[b] * (cotangents[b] * gain_h) - seconds[b] * attended[b] for b in blocks
+        ]
+        sides = [jnp.concatenate(split(grads[b] * starts[b]), axis=1) for b in blocks]
+        mine = [halves(dot(query_blocks[b], sides[b], 0, 0)) for b in blocks]
+        normed = [attended[b] * scales[b] for b in blocks]
+        for b in reversed(blocks):
+            part = part + jnp.sum(cotangents[b] * normed[b], axis=0, keepdims=True)
+            state = factors[b] * state + mine[b]
+        for b in blocks:
+            at = spans[b]
+            out[at, cols(h)] = (normed[b] * gain_h).astype(bf16)
+            attn[at, cols(h)] = grads[b]
+            back[h, b] = mine[b]
         gparts[z, :, cols(h)] = part
         b_out[h] = state
         store(0, h).start()
@@ -248,30 +277,38 @@
         backward(h).start()
 
     def inside_gradients(h):
-        for b in range(count):
-            at = pl.ds(b * size, size)
-            query, key, value = q[at, cols(h)], k[at, cols(h)], v[at, cols(h)]
-            a_high, a_low = split(attn[at, cols(h)])
-            a_both = jnp.concatenate([a_high, a_low], axis=1)
-            e_high, e_low = split(entering[h, b])
-            right = jnp.concatenate(
-                [jnp.concatenate([value, value], axis=1), jnp.concatenate([e_high, e_high], axis=1)], axis=0
-            )
-            both = dot(a_both, right, 1, 1)
-            ds_high, ds_low = split(both[:, :size] * mask[h, at, :])
-            cross = both[:, size:] + dot(a_high, e_low, 1, 1)
-            dq[at, cols(h)] = (
-                dot(jnp.concatenate([ds_high, ds_low], axis=1), jnp.concatenate([key, key], axis=0))
-                + cols_g[at, cols(h)] * cross
-            ).astype(bf16)
-            mask[h, at, :] = dot(
-                jnp.concatenate([ds_high, ds_low], axis=0), jnp.concatenate([query, query], axis=0), 0, 0
-            )
-            right = jnp.concatenate(
-                [a_both, jnp.concatenate([a_high, jnp.zeros_like(a_high)], axis=1)], axis=0
-            )
-            both = dot(jnp.concatenate([p_high[h, at, :], p_low[h, at, :]], axis=1), right)
-            attn[at, cols(h)] = both[:, :WIDTH] + both[:, WIDTH:]
+        query_blocks = [q[at, cols(h)] for at in spans]
+        key_blocks = [k[at, cols(h)] for at in spans]
+        value_blocks = [v[at, cols(h)] for at in spans]
+        parts = [split(attn[at, cols(h)]) for at in spans]
+        masks = [mask[h, at, :] for at in spans]
+        starts = [cols_g[at, cols(h)] for at in spans]
+        states_in = [split(entering[h, b]) for b in blocks]
+        highs = [p_high[h, at, :] for at in spans]
+        lows = [p_low[h, at, :] for at in spans]
+        both = [jnp.concatenate(parts[b], axis=1) for b in blocks]
+        score_grads = [
+            split(dot(both[b], jnp.concatenate([value_blocks[b]] * 2, axis=1), 1, 1) * masks[b]) for b in blocks
+        ]
+        crosses = [
+            dot(both[b], jnp.concatenate([states_in[b][0]] * 2, axis=1), 1, 1)
+            + dot(parts[b][0], states_in[b][1], 1, 1)
+            for b in blocks
+        ]
+        value_parts = [halves(dot(highs[b], both[b])) + dot(lows[b], parts[b][0]) for b in blocks]
+        query_parts = [
+            dot(score_grads[b][0], key_blocks[b]) + dot(score_grads[b][1], key_blocks[b]) + starts[b] * crosses[b]
+            for b in blocks
+        ]
+        key_parts = [
+            dot(score_grads[b][0], query_blocks[b], 0, 0) + dot(score_grads[b][1], query_blocks[b], 0, 0)
+            for b in blocks
+        ]
+        for b in blocks:
+            at = spans[b]
+            dq[at, cols(h)] = query_parts[b].astype(bf16)
+            mask[h, at, 0:WIDTH] = key_parts[b]
+            attn[at, cols(h)] = value_parts[b]
         store(1, h).start()
 
     def leave(h):
@@ -280,16 +317,27 @@
             backward(h).wait_recv()
 
         state = b_in[h]
-        for b in reversed(range(count)):
-            at = pl.ds(b * size, size)
-            key, value = k[at, cols(h)], v[at, cols(h)]
-            to_end = ends[at, cols(h)]
-            s_high, s_low = split(state)
-            from_later = dot(jnp.concatenate([value, value], axis=1), jnp.concatenate([s_high, s_low], axis=1), 1, 1)
-            dk[at, cols(h)] = (mask[h, at, :] + to_end * from_later).astype(bf16)
-            from_later = dot(jnp.concatenate([key, key], axis=1), jnp.concatenate([s_high, s_low], axis=0))
-            dv[at, cols(h)] = (attn[at, cols(h)] + to_end * from_later).astype(bf16)
-            state = factor(h, b) * state + back[h, b]
+        factors = [factor(h, b) for b in blocks]
+        back_blocks = [back[h, b] for b in blocks]
+        key_blocks = [k[at, cols(h)] for at in spans]
+        value_blocks = [v[at, cols(h)] for at in spans]
+        to_ends = [ends[at, cols(h)] for at in spans]
+        key_parts = [mask[h, at, 0:WIDTH] for at in spans]
+        value_parts = [attn[at, cols(h)] for at in spans]
+        after = [None] * count
+        for b in reversed(blocks):
+            after[b] = split(state)
+            state = factors[b] * state + back_blocks[b]
+        from_values = [
+            dot(jnp.concatenate([value_blocks[b]] * 2, axis=1), jnp.concatenate(after[b], axis=1), 1, 1) for b in blocks
+        ]
+        from_keys = [
+            dot(jnp.concatenate([key_blocks[b]] * 2, axis=1), jnp.concatenate(after[b], axis=0)) for b in blocks
+        ]
+        for b in blocks:
+            at = spans[b]
+            dk[at, cols(h)] = (key_parts[b] + to_ends[b] * from_values[b]).astype(bf16)
+            dv[at, cols(h)] = (value_parts[b] + to_ends[b] * from_keys[b]).astype(bf16)
         store(2, h).start()
         store(3, h).start()
 
@@ -341,11 +389,27 @@
             backward(h).wait_send()
 
 
+def hand_on(rows, *refs):
+    sources, targets, sem = refs[:5], refs[5:10], refs[10]
+    pieces = 8
+    step = rows // pieces
+    copies = []
+    for n in range(4):
+        for p in range(pieces):
+            at = pl.ds(p * step, step)
+            copies.append(pltpu.make_async_copy(sources[n].at[at], targets[n].at[at], sem.at[n, p]))
+    for copy in copies:
+        copy.start()
+    targets[4][...] = sources[4][...]
+    for copy in copies:
+        copy.wait()
+
+
 def local(queries, keys, values, log_decay, gain, out_grad):
     rows, channels = queries.shape
     heads = log_decay.shape[0]
     seq_count, head_count = lax.axis_size("seq"), lax.axis_size("head")
-    size = min(128, rows)
+    size = min(256, rows)
     count = rows // size
     any_spec = pl.BlockSpec(memory_space=pl.ANY)
     vmem_spec = pl.BlockSpec(memory_space=pltpu.VMEM)
@@ -384,6 +448,15 @@
         ),
         name="lightning",
     )(log_decay, gain.reshape(1, channels), queries, keys, values, out_grad)
+    results = pl.pallas_call(
+        functools.partial(hand_on, rows),
+        out_shape=(narrow,) * 4 + (jax.ShapeDtypeStruct((1, channels), f32),),
+        in_specs=[any_spec] * 4 + [vmem_spec],
+        out_specs=(any_spec,) * 4 + (vmem_spec,),
+        scratch_shapes=[dma((4, 8))],
+        compiler_params=pltpu.CompilerParams(vmem_limit_bytes=60 * 1024 * 1024),
+        name="hand_on",
+    )(*results)
     return results[:4] + (results[4].reshape(channels),)
 
 

time: 75.5 us -> 315 us (4.17)
  Pallas kernels: 63.5 us -> 315 us
  local copies, waits for them, and re-layouts: 9.84 us -> 0 us
    pallas_call x0 -> x1, Pallas kernels: none -> 257 us  [local(): pl.pallas_call(functools.partial(hand_on, rows), out_shape=(narrow,) * 4...]
    unnamed x13 -> x0, local copies, waits for them, and re-layouts: 9.84 us -> none
    pallas_call x1, Pallas kernels: 63.5 us -> 57.8 us  [local(): pl.pallas_call(functools.partial(kernel, seq_count, head_count, heads, ro...]
where the time goes in v4:
time: 315 us
  Pallas kernels  315 us (100%)
    pallas_call x1, Pallas kernels, local(): pl.pallas_call(functools.partial(hand_on, rows), out_shape=(narrow,) * 4...  257 us
    pallas_call x1, Pallas kernels, local(): pl.pallas_call(functools.partial(kernel, seq_count, head_count, heads, ro...  57.8 us

profile of v4, /device:TPU:0, one launch (start us, length us, event | category | flops | bytes accessed | tf_op | source)
XLA Modules:
  0.0 315.2 jit_solution(2200820438987089126)
XLA Ops:
  0.6 57.8 %lightning.1 = (bf16[1024,1024]{1,0:T(8,128)(2,1)}, bf16[1024,1024]{1,0:T(8,128)(2,1)}, bf16[1024,1024]{1,0:T(8,128)(2,1)}, bf16[1024,1024]{1,0:T(8,128)(2,1)}, f32[1,1024]{1,0:T(1,128)}) custom-call(f32[8,1024]{1,0:T(8,128)} %decay.1, f32[1,1024]{1,0:T(1,128)} %bitcast.2, bf16[1024,1024]{1,0:T(8,128)(2,1)} %q_hbm.1, bf16[1024,1024]{1,0:T(8,128)(2,1)} %k_hbm.1, ...), custom_call_target="tpu_custom_call" | custom-call | tf_op jit(solution)/shard_map/lightning/pallas_call | solution.py:420
  58.4 256.8 %hand_on.1 = (bf16[1024,1024]{1,0:T(8,128)(2,1)}, bf16[1024,1024]{1,0:T(8,128)(2,1)}, bf16[1024,1024]{1,0:T(8,128)(2,1)}, bf16[1024,1024]{1,0:T(8,128)(2,1)}, f32[1,1024]{1,0:T(1,128)}) custom-call(bf16[1024,1024]{1,0:T(8,128)(2,1)} %get-tuple-element.15.refs_0_, bf16[1024,1024]{1,0:T(8,128)(2,1)} %get-tuple-element.16.refs_1_, ...), custom_call_target="tpu_custom_call" | custom-call | tf_op jit(solution)/shard_map/hand_on/pallas_call | solution.py:451

commit v5 on v4

--- a/solution.py
+++ b/solution.py
@@ -29,7 +29,7 @@
     out_hbm, dq_hbm, dk_hbm, dv_hbm, dgain,
     q, k, v, g, out, dq, dk, dv,
     attn, sums_g, cols_g, ends, own, entering, back, mask, p_high, p_low,
-    f_in, f_out, b_in, b_out, acc_sq, acc_pr, norm, alpha, beta, gparts,
+    decays, f_in, f_out, b_in, b_out, acc_sq, acc_pr, norm, alpha, beta, gparts,
     in_sem, out_sem, f_send, f_recv, b_send, b_recv, n_send, n_recv, g_send, g_recv,
 ):
     z = lax.axis_index("seq")
@@ -111,6 +111,10 @@
             ends[spans[b], cols(h)] = to_ends[b]
             own[h, b] = mine[b]
         f_out[h] = state
+        whole = jnp.exp(lasts[0])
+        for b in range(1, count):
+            whole = whole * jnp.exp(lasts[b])
+        decays[h] = whole
 
         @pl.when(z == 0)
         def _():
@@ -121,10 +125,7 @@
     lax.fori_loop(0, heads, states, 0)
 
     def device_factor(h):
-        result = factor(h, 0)
-        for b in range(1, count):
-            result = result * factor(h, b)
-        return result
+        return decays[h]
 
     def attend(h):
         load(2, h).wait()
@@ -149,15 +150,15 @@
             attn[at, cols(h)] = inside[b]
             cols_g[at, cols(h)] = jnp.exp(columns[b])
 
-    def enter(h):
-        @pl.when(z > 0)
+    def pass_forward(h):
+        forward(h).wait_recv()
+        f_out[h] = f_out[h] + device_factor(h) * f_in[h]
+        forward(h).start()
+
+    def enter(h, carry):
+        @pl.when(z == seq_count - 1)
         def _():
             forward(h).wait_recv()
-
-            @pl.when(z < seq_count - 1)
-            def _():
-                f_out[h] = f_out[h] + device_factor(h) * f_in[h]
-                forward(h).start()
 
         state = f_in[h]
         factors = [factor(h, b) for b in blocks]
@@ -182,19 +183,23 @@
             acc_sq[at, :] = acc_sq[at, :] + results[b] * results[b]
             acc_pr[at, :] = acc_pr[at, :] + results[b] * weights[b]
 
-    lag = jnp.where(z == 0, 0, jnp.minimum(heads, 3 * z - 1))
+        return carry
+
+    between = jnp.logical_and(z > 0, z < seq_count - 1)
+    lag = jnp.where(between, jnp.minimum(heads, z - 1), 0)
 
     def forward_step(i, carry):
+        @pl.when(jnp.logical_and(between, i >= lag))
+        def _():
+            pass_forward(i - lag)
+
         @pl.when(i < heads)
         def _():
             attend(i)
-
-        @pl.when(i >= lag)
-        def _():
-            enter(i - lag)
         return carry
 
     lax.fori_loop(0, heads + lag, forward_step, 0)
+    lax.fori_loop(0, heads, enter, 0)
 
     for b in range(rows // WIDTH):
         at = pl.ds(b * WIDTH, WIDTH)
@@ -311,7 +316,7 @@
             attn[at, cols(h)] = value_parts[b]
         store(1, h).start()
 
-    def leave(h):
+    def leave(h, carry):
         @pl.when(z == 0)
         def _():
             backward(h).wait_recv()
@@ -340,9 +345,9 @@
             dv[at, cols(h)] = (value_parts[b] + to_ends[b] * from_keys[b]).astype(bf16)
         store(2, h).start()
         store(3, h).start()
-
-    late = jnp.where(z == seq_count - 1, 0, jnp.minimum(heads, 1 + 2 * (seq_count - 2 - z)))
-    between = jnp.logical_and(z > 0, z < seq_count - 1)
+        return carry
+
+    late = jnp.where(between, jnp.minimum(heads, 1 + 3 * (seq_count - 2 - z)), 0)
 
     def backward_step(i, carry):
         for r in range(2):
@@ -355,13 +360,10 @@
         @pl.when(i < heads)
         def _():
             inside_gradients(i)
-
-        @pl.when(i >= late)
-        def _():
-            leave(i - late)
         return carry
 
     lax.fori_loop(0, heads + late, backward_step, 0)
+    lax.fori_loop(0, heads, leave, 0)
 
     for step in range(1, seq_count):
         gain_copy(step, lax.rem(z + seq_count - step, seq_count)).wait_recv()
@@ -390,18 +392,22 @@
 
 
 def hand_on(rows, *refs):
-    sources, targets, sem = refs[:5], refs[5:10], refs[10]
+    sources, targets, held, in_sem, out_sem = refs[:5], refs[5:10], refs[10:14], refs[14], refs[15]
     pieces = 8
     step = rows // pieces
-    copies = []
-    for n in range(4):
-        for p in range(pieces):
+    arriving, leaving = [], []
+    for p in range(pieces):
+        for n in range(4):
             at = pl.ds(p * step, step)
-            copies.append(pltpu.make_async_copy(sources[n].at[at], targets[n].at[at], sem.at[n, p]))
-    for copy in copies:
+            arriving.append(pltpu.make_async_copy(sources[n].at[at], held[n].at[at], in_sem.at[n, p]))
+            leaving.append(pltpu.make_async_copy(held[n].at[at], targets[n].at[at], out_sem.at[n, p]))
+    for copy in arriving:
         copy.start()
     targets[4][...] = sources[4][...]
-    for copy in copies:
+    for first, second in zip(arriving, leaving):
+        first.wait()
+        second.start()
+    for copy in leaving:
         copy.wait()
 
 
@@ -432,6 +438,7 @@
             pltpu.VMEM((heads, rows, size), f32),
             pltpu.VMEM((heads, rows, size), bf16),
             pltpu.VMEM((heads, rows, size), bf16),
+            pltpu.VMEM((heads, 1, WIDTH), f32),
             state, state, state, state,
             pltpu.VMEM((rows, WIDTH), f32),
             pltpu.VMEM((rows, WIDTH), f32),
@@ -453,7 +460,7 @@
         out_shape=(narrow,) * 4 + (jax.ShapeDtypeStruct((1, channels), f32),),
         in_specs=[any_spec] * 4 + [vmem_spec],
         out_specs=(any_spec,) * 4 + (vmem_spec,),
-        scratch_shapes=[dma((4, 8))],
+        scratch_shapes=[pltpu.VMEM((rows, channels), bf16)] * 4 + [dma((4, 8)), dma((4, 8))],
         compiler_params=pltpu.CompilerParams(vmem_limit_bytes=60 * 1024 * 1024),
         name="hand_on",
     )(*results)

time: 315 us -> 65.7 us (0.21)
  Pallas kernels: 315 us -> 64.8 us
    pallas_call x1, Pallas kernels: 257 us -> 8.29 us  [local(): pl.pallas_call(functools.partial(hand_on, rows), out_shape=(narrow,) * 4...]
where the time goes in v5:
time: 65.7 us; the launch traced here: 65.4 us
  Pallas kernels  64.8 us (99%)
    pallas_call x1, Pallas kernels, local(): pl.pallas_call(functools.partial(kernel, seq_count, head_count, heads, ro...  56.5 us
    pallas_call x1, Pallas kernels, local(): pl.pallas_call(functools.partial(hand_on, rows), out_shape=(narrow,) * 4...  8.29 us

profile of v5, /device:TPU:0, one launch (start us, length us, event | category | flops | bytes accessed | tf_op | source)
XLA Modules:
  0.0 65.4 jit_solution(15200521112271822548)
XLA Ops:
  0.6 56.5 %lightning.1 = (bf16[1024,1024]{1,0:T(8,128)(2,1)}, bf16[1024,1024]{1,0:T(8,128)(2,1)}, bf16[1024,1024]{1,0:T(8,128)(2,1)}, bf16[1024,1024]{1,0:T(8,128)(2,1)}, f32[1,1024]{1,0:T(1,128)}) custom-call(f32[8,1024]{1,0:T(8,128)} %decay.1, f32[1,1024]{1,0:T(1,128)} %bitcast.2, bf16[1024,1024]{1,0:T(8,128)(2,1)} %q_hbm.1, bf16[1024,1024]{1,0:T(8,128)(2,1)} %k_hbm.1, ...), custom_call_target="tpu_custom_call" | custom-call | tf_op jit(solution)/shard_map/lightning/pallas_call | solution.py:426
  57.2 8.3 %hand_on.1 = (bf16[1024,1024]{1,0:T(8,128)(2,1)}, bf16[1024,1024]{1,0:T(8,128)(2,1)}, bf16[1024,1024]{1,0:T(8,128)(2,1)}, bf16[1024,1024]{1,0:T(8,128)(2,1)}, f32[1,1024]{1,0:T(1,128)}) custom-call(bf16[1024,1024]{1,0:T(8,128)(2,1)} %get-tuple-element.15.refs_0_, bf16[1024,1024]{1,0:T(8,128)(2,1)} %get-tuple-element.16.refs_1_, ...), custom_call_target="tpu_custom_call" | custom-call | tf_op jit(solution)/shard_map/hand_on/pallas_call | solution.py:458

commit v6 on v5

--- a/solution.py
+++ b/solution.py
@@ -34,7 +34,7 @@
 ):
     z = lax.axis_index("seq")
     me = lax.axis_index("head")
-    size = min(256, rows)
+    size = min(128, rows)
     count = rows // size
     channels = heads * WIDTH * head_count
 
@@ -141,7 +141,9 @@
             for b in blocks
         ]
         parts = [split(scores[b] * masks[b]) for b in blocks]
-        inside = [dot(parts[b][0], value_blocks[b]) + dot(parts[b][1], value_blocks[b]) for b in blocks]
+        inside = [
+            dot(jnp.concatenate(parts[b], axis=1), jnp.concatenate([value_blocks[b]] * 2, axis=0)) for b in blocks
+        ]
         for b in blocks:
             at = spans[b]
             mask[h, at, :] = masks[b]
@@ -292,21 +294,29 @@
         highs = [p_high[h, at, :] for at in spans]
         lows = [p_low[h, at, :] for at in spans]
         both = [jnp.concatenate(parts[b], axis=1) for b in blocks]
-        score_grads = [
-            split(dot(both[b], jnp.concatenate([value_blocks[b]] * 2, axis=1), 1, 1) * masks[b]) for b in blocks
-        ]
-        crosses = [
-            dot(both[b], jnp.concatenate([states_in[b][0]] * 2, axis=1), 1, 1)
-            + dot(parts[b][0], states_in[b][1], 1, 1)
-            for b in blocks
-        ]
-        value_parts = [halves(dot(highs[b], both[b])) + dot(lows[b], parts[b][0]) for b in blocks]
+        rights = [
+            jnp.concatenate(
+                [jnp.concatenate([value_blocks[b]] * 2, axis=1), jnp.concatenate([states_in[b][0]] * 2, axis=1)], axis=0
+            )
+            for b in blocks
+        ]
+        products = [dot(both[b], rights[b], 1, 1) for b in blocks]
+        rest = [dot(parts[b][0], states_in[b][1], 1, 1) for b in blocks]
+        score_grads = [split(products[b][:, :size] * masks[b]) for b in blocks]
+        rights = [
+            jnp.concatenate(
+                [both[b], jnp.concatenate([parts[b][0], jnp.zeros_like(parts[b][0])], axis=1)], axis=0
+            )
+            for b in blocks
+        ]
+        value_parts = [halves(dot(jnp.concatenate([highs[b], lows[b]], axis=1), rights[b])) for b in blocks]
         query_parts = [
-            dot(score_grads[b][0], key_blocks[b]) + dot(score_grads[b][1], key_blocks[b]) + starts[b] * crosses[b]
+            dot(jnp.concatenate(score_grads[b], axis=1), jnp.concatenate([key_blocks[b]] * 2, axis=0))
+            + starts[b] * (products[b][:, size:] + rest[b])
             for b in blocks
         ]
         key_parts = [
-            dot(score_grads[b][0], query_blocks[b], 0, 0) + dot(score_grads[b][1], query_blocks[b], 0, 0)
+            dot(jnp.concatenate(score_grads[b], axis=0), jnp.concatenate([query_blocks[b]] * 2, axis=0), 0, 0)
             for b in blocks
         ]
         for b in blocks:
@@ -415,7 +425,7 @@
     rows, channels = queries.shape
     heads = log_decay.shape[0]
     seq_count, head_count = lax.axis_size("seq"), lax.axis_size("head")
-    size = min(256, rows)
+    size = min(128, rows)
     count = rows // size
     any_spec = pl.BlockSpec(memory_space=pl.ANY)
     vmem_spec = pl.BlockSpec(memory_space=pltpu.VMEM)

time: 65.7 us -> 65.9 us (level)
  no operation moved by 1% of the time
where the time goes in v6:
time: 65.9 us; the launch traced here: 65.6 us
  Pallas kernels  65 us (99%)
    pallas_call x1, Pallas kernels, local(): pl.pallas_call(functools.partial(kernel, seq_count, head_count, heads, ro...  56.7 us
    pallas_call x1, Pallas kernels, local(): pl.pallas_call(functools.partial(hand_on, rows), out_shape=(narrow,) * 4...  8.29 us

profile of v6, /device:TPU:0, one launch (start us, length us, event | category | flops | bytes accessed | tf_op | source)
XLA Modules:
  0.0 65.6 jit_solution(5061192155327964141)
XLA Ops:
  0.6 56.7 %lightning.1 = (bf16[1024,1024]{1,0:T(8,128)(2,1)}, bf16[1024,1024]{1,0:T(8,128)(2,1)}, bf16[1024,1024]{1,0:T(8,128)(2,1)}, bf16[1024,1024]{1,0:T(8,128)(2,1)}, f32[1,1024]{1,0:T(1,128)}) custom-call(f32[8,1024]{1,0:T(8,128)} %decay.1, f32[1,1024]{1,0:T(1,128)} %bitcast.2, bf16[1024,1024]{1,0:T(8,128)(2,1)} %q_hbm.1, bf16[1024,1024]{1,0:T(8,128)(2,1)} %k_hbm.1, ...), custom_call_target="tpu_custom_call" | custom-call | tf_op jit(solution)/shard_map/lightning/pallas_call | solution.py:436
  57.4 8.3 %hand_on.1 = (bf16[1024,1024]{1,0:T(8,128)(2,1)}, bf16[1024,1024]{1,0:T(8,128)(2,1)}, bf16[1024,1024]{1,0:T(8,128)(2,1)}, bf16[1024,1024]{1,0:T(8,128)(2,1)}, f32[1,1024]{1,0:T(1,128)}) custom-call(bf16[1024,1024]{1,0:T(8,128)(2,1)} %get-tuple-element.15.refs_0_, bf16[1024,1024]{1,0:T(8,128)(2,1)} %get-tuple-element.16.refs_1_, ...), custom_call_target="tpu_custom_call" | custom-call | tf_op jit(solution)/shard_map/hand_on/pallas_call | solution.py:468
